TPU v7x, 32 devices: a whole 2x2x4 slice. The times are simulated.
32 devices in a mesh: tm: 4 (over y, x), space: 4 (over z), ens: 2 (over core).
Axes of the slice: x: 2, y: 2, z: 4, core: 2. Of those that a mesh axis runs over, the one named last changes fastest.
Arguments:
- start_states: float32 [4, 16, 256, 1024], P('tm', 'ens', 'space'), may hold values from -6 to 6
- velocity_x: float32 [256, 1024], P('space'), may hold values from -0.15 to 0.15
- velocity_y: float32 [256, 1024], P('space'), may hold values from -0.15 to 0.15
- diffusivity: float32 [256, 1024], P('space'), may hold values from 0.06 to 0.2
- source_shape: float32 [256, 1024], P('space'), may hold values from -6 to 6
- params: float32 [16, 128], P('ens'), may hold values from -6 to 6
- obs_cell: int32 [4, 256], P('tm', 'space'), may hold values from 0 to 262143, as said below
- obs_data: float32 [4, 256], P('tm', 'space'), may hold values from -6 to 6
- obs_noise: float32 [4, 256, 16], P('tm', 'space'), may hold values from -6 to 6
- obs_var: float32 [4, 256], P('tm', 'space'), may hold values from 0.05 to 0.5
Outputs:
- new_states: float32 [4, 16, 256, 1024], P('tm', 'ens', 'space')
- new_params: float32 [16, 128], P('ens')
Inputs may be any that keep to these rules, and one draw needn't show every extreme that they name: `obs_cell`: entry (n, o) lies in the rows of slab o // 64, that is row (o // 64) * 64 up to 63 rows further.
All inputs are finite; a program needn't handle non-finite values.
Results may differ from a plain program's by a relative error of at most 0.0003.
Values sent between devices are 32-bit elements; how exact they have to be, the bound alone decides.
A program may use at most 128 MiB of HBM per device.

v0:
```python
import math

import jax
import jax.numpy as jnp
from jax import lax
from jax.sharding import PartitionSpec as P

FINE = 4


FINE_DT = 0.25


def with_halo(cells, sides, width):
    for axis, dim in sides:
        count = lax.axis_size(axis)
        ends = count - 1
        head = lax.slice_in_dim(cells, 0, width, axis=dim)
        tail = lax.slice_in_dim(cells, cells.shape[dim] - width, cells.shape[dim], axis=dim)
        cells = jnp.concatenate(
            [
                lax.ppermute(tail, axis, [(i, (i + 1) % count) for i in range(ends)]),
                cells,
                lax.ppermute(head, axis, [((i + 1) % count, i) for i in range(ends)]),
            ],
            axis=dim,
        )
    return cells


def shifted(value, axis, steps):
    count = lax.axis_size(axis)
    first, last = (max(0, -steps), min(count, count - steps))
    return lax.ppermute(value, axis, [(source, source + steps) for source in range(first, last)])


def advance(values_in, coeffs, inside, step_size, forcing):
    middle = values_in[:, 1:-1, :]
    above_row = values_in[:, :-2, :]
    below_row = values_in[:, 2:, :]
    west_cell = jnp.pad(middle[:, :, :-1], ((0, 0), (0, 0), (1, 0)))
    east_cell = jnp.pad(middle[:, :, 1:], ((0, 0), (0, 0), (0, 1)))
    spread_term = coeffs[0] * (above_row + below_row + west_cell + east_cell - 4.0 * middle)
    tendency = (
        spread_term
        - coeffs[1] * (east_cell - west_cell) * 0.5
        - coeffs[2] * (below_row - above_row) * 0.5
    )
    if forcing is not None:
        tendency = tendency + forcing
    return (middle + step_size * tendency) * inside


def row_inside(first_row, count, total_rows):
    global_rows = first_row + jnp.arange(count, dtype=jnp.int32)
    return ((global_rows >= 0) & (global_rows < total_rows)).astype(jnp.float32)[:, None]


def per_device(
    start_states,
    velocity_x,
    velocity_y,
    diffusivity,
    source_shape,
    params,
    obs_cell,
    obs_data,
    obs_noise,
    obs_var,
):
    coarse_dt = FINE_DT * FINE
    state = start_states[0]
    members_here, row_count, col_count = state.shape
    slabs = row_count * lax.axis_size("space")
    first_row = lax.axis_index("space") * row_count
    slice_index = lax.axis_index("tm")
    band_width = col_count // params.shape[1]
    spread_params = jnp.repeat(params, band_width, axis=1)
    coeffs = jnp.stack([diffusivity, velocity_x, velocity_y])
    own_rows = row_inside(first_row, row_count, slabs)
    forcing = source_shape[None] * spread_params[:, None, :]
    current = state
    coarse_part = state
    for section in range(FINE):
        padded = with_halo(current, (("space", 1),), 1)
        if section == 0:
            coarse_part = advance(padded, coeffs, own_rows, coarse_dt, None)
        current = advance(padded, coeffs, own_rows, FINE_DT, forcing)
    correction = jnp.where(slice_index > 0, current - coarse_part, current)
    running = correction
    for link in range(lax.axis_size("tm") - 1):
        earlier = shifted(running, "tm", 1)
        padded = with_halo(earlier, (("space", 1),), 1)
        running = correction + advance(padded, coeffs, own_rows, coarse_dt, None)
    new_states = running[None]
    flat = running.reshape(members_here, row_count * col_count)
    local_cell = obs_cell[0] - first_row * col_count
    predicted = jnp.take(flat, local_cell, axis=1)
    every_pred, every_param = (
        lax.all_gather(predicted, "ens", axis=0, tiled=True),
        lax.all_gather(params, "ens", axis=0, tiled=True),
    )
    total = every_pred.shape[0]
    norm_factor = 1.0 / math.sqrt(total - 1)
    inv_spread = lax.rsqrt(obs_var[0])[None, :]
    pred_mean = jnp.mean(every_pred, axis=0, keepdims=True)
    anomaly = (every_pred - pred_mean) * (inv_spread * norm_factor)
    misfit = (obs_data[0][None, :] + obs_noise[0].T - every_pred) * inv_spread
    gram = jnp.dot(anomaly, anomaly.T, precision=lax.Precision.HIGHEST)
    cross = jnp.dot(anomaly, misfit.T, precision=lax.Precision.HIGHEST)
    gram, cross = lax.psum((gram, cross), ("tm", "space"))
    system = jnp.eye(total, dtype=jnp.float32) + gram
    factor = jnp.linalg.cholesky(system)
    weights = jax.scipy.linalg.cho_solve((factor, True), cross)
    param_anom = every_param - jnp.mean(every_param, axis=0)
    own_weights = lax.dynamic_slice_in_dim(
        weights, lax.axis_index("ens") * members_here, members_here, 1
    )
    new_params = (
        params + jnp.dot(own_weights.T, param_anom, precision=lax.Precision.HIGHEST) * norm_factor
    )
    return (new_states, new_params)


def solution(mesh):
    in_specs = (
        P("tm", "ens", "space", None),
        P("space", None),
        P("space", None),
        P("space", None),
        P("space", None),
        P("ens", None),
        P("tm", "space"),
        P("tm", "space"),
        P("tm", "space", None),
        P("tm", "space"),
    )
    out_specs = (P("tm", "ens", "space", None), P("ens", None))
    return jax.shard_map(
        per_device, mesh=mesh, in_specs=in_specs, out_specs=out_specs, check_vma=False
    )
```

profile of v0, /device:TPU:0, one launch (start us, length us, event | category | flops | bytes accessed | tf_op | source)
XLA Modules:
  0.0 328.9 jit_solution(7530201876869984689)
XLA Ops:
  1.7 4.9 %collective-permute-start = (f32[8,1,1024]{2,1,0:T(1,128)S(1)}, f32[8,1,1024]{2,1,0:T(1,128)S(1)}, u32[]{:S(2)}, u32[]{:S(2)}) collective-permute-start(f32[8,1,1024]{2,1,0:T(1,128)S(1)} %get-tuple-element.31), channel_id=1, source_target_pairs={{0,2},{2,4},{4,6},{1,3},{3,5},{5,7},{8,10},{10,12},{12,14},{9,11},... | collective-permute-start | bytes 98312 | tf_op jit(solution)/shard_map/ppermute | solution.py:22
  8.0 5.1 %fusion.52 = (f32[8,64,1023]{2,1,0:T(8,128)}, f32[8,64,1023]{2,1,0:T(8,128)}) fusion(f32[8,64,1024]{2,1,0:T(8,128)} %bitcast.40), kind=kLoop, calls=%fused_computation.96 | loop fusion | bytes 8380416 | tf_op jit(solution)/shard_map/slice | solution.py:41
  15.6 3.4 %fusion.2 = f32[8,64,1024]{2,1,0:T(8,128)S(1)} fusion(f32[8,64,1024]{2,1,0:T(8,128)S(1)} %bitcast.41, f32[8,1,1024]{2,1,0:T(1,128)S(1)} %collective-permute-done, f32[8,1,1024]{2,1,0:T(1,128)S(1)} %collective-permute-done.1, f32[64]{0:T(128)S(1)} %and_convert_fusion, f32[8,1024]{1,0:T(8,128)S(1)} %mul.162, f32[64,1024]{1,0:T(8,128)S(1)} %copy-done.8, ...), kind=kLoop, calls=%fused_computation.8 | loop fusion | flops 11010048 | bytes 9531648 | tf_op jit(solution)/shard_map/mul | solution.py:51
  19.1 4.5 %collective-permute-start.2 = (f32[8,1,1024]{2,1,0:T(1,128)S(1)}, f32[8,1,1024]{2,1,0:T(1,128)S(1)}, u32[]{:S(2)}, u32[]{:S(2)}) collective-permute-start(f32[8,1,1024]{2,1,0:T(1,128)S(1)} %get-tuple-element.25), channel_id=1, source_target_pairs={{0,2},{2,4},{4,6},{1,3},{3,5},{5,7},{8,10},{10,12},{12,14},{9,11},... | collective-permute-start | bytes 98312 | tf_op jit(solution)/shard_map/ppermute | solution.py:22
  25.8 3.7 %collective-permute-done.3 = f32[8,1,1024]{2,1,0:T(1,128)S(1)} collective-permute-done((f32[8,1,1024]{2,1,0:T(1,128)S(1)}, f32[8,1,1024]{2,1,0:T(1,128)S(1)}, u32[]{:S(2)}, u32[]{:S(2)}) %collective-permute-start.3) | collective-permute-done | bytes 32800 | tf_op jit(solution)/shard_map/ppermute | solution.py:24
  31.6 3.5 %collective-permute-start.4 = (f32[8,1,1024]{2,1,0:T(1,128)S(1)}, f32[8,1,1024]{2,1,0:T(1,128)S(1)}, u32[]{:S(2)}, u32[]{:S(2)}) collective-permute-start(f32[8,1,1024]{2,1,0:T(1,128)S(1)} %get-tuple-element.21), channel_id=1, source_target_pairs={{0,2},{2,4},{4,6},{1,3},{3,5},{5,7},{8,10},{10,12},{12,14},{9,11},... | collective-permute-start | bytes 98312 | tf_op jit(solution)/shard_map/ppermute | solution.py:22
  37.2 3.7 %collective-permute-done.5 = f32[8,1,1024]{2,1,0:T(1,128)S(1)} collective-permute-done((f32[8,1,1024]{2,1,0:T(1,128)S(1)}, f32[8,1,1024]{2,1,0:T(1,128)S(1)}, u32[]{:S(2)}, u32[]{:S(2)}) %collective-permute-start.5) | collective-permute-done | bytes 32800 | tf_op jit(solution)/shard_map/ppermute | solution.py:24
  43.0 3.5 %collective-permute-start.6 = (f32[8,1,1024]{2,1,0:T(1,128)S(1)}, f32[8,1,1024]{2,1,0:T(1,128)S(1)}, u32[]{:S(2)}, u32[]{:S(2)}) collective-permute-start(f32[8,1,1024]{2,1,0:T(1,128)S(1)} %get-tuple-element.17), channel_id=1, source_target_pairs={{0,2},{2,4},{4,6},{1,3},{3,5},{5,7},{8,10},{10,12},{12,14},{9,11},... | collective-permute-start | bytes 98312 | tf_op jit(solution)/shard_map/ppermute | solution.py:22
  48.9 3.7 %collective-permute-done.7 = f32[8,1,1024]{2,1,0:T(1,128)S(1)} collective-permute-done((f32[8,1,1024]{2,1,0:T(1,128)S(1)}, f32[8,1,1024]{2,1,0:T(1,128)S(1)}, u32[]{:S(2)}, u32[]{:S(2)}) %collective-permute-start.7) | collective-permute-done | bytes 32800 | tf_op jit(solution)/shard_map/ppermute | solution.py:24
  52.6 4.7 %subtract_select_fusion = f32[8,64,1024]{2,1,0:T(8,128)S(1)} fusion(f32[8,64,1024]{2,1,0:T(8,128)S(1)} %fusion.8, f32[8,64,1024]{2,1,0:T(8,128)S(1)} %bitcast.42, f32[8,64,1023]{2,1,0:T(8,128)S(1)} %get-tuple-element.19, f32[8,64,1023]{2,1,0:T(8,128)S(1)} %get-tuple-element.18, f32[8,1,1024]{2,1,0:T(1,128)S(1)} %collective-permute-done.6, ...), kind=kLoop, calls=%fused_computation.5 | loop fusion | flops 21495808 | bytes 15884545 | tf_op jit(solution)/shard_map/jit(_where)/select_n | solution.py:89
  57.3 3.5 %collective-permute-start.8 = (f32[8,64,1024]{2,1,0:T(8,128)S(1)}, f32[8,64,1024]{2,1,0:T(8,128)S(1)}, u32[]{:S(2)}, u32[]{:S(2)}) collective-permute-start(f32[8,64,1024]{2,1,0:T(8,128)S(1)} %subtract_select_fusion), channel_id=1, source_target_pairs={{0,8},{8,16},{16,24},{1,9},{9,17},{17,25},{2,10},{10,18},{18,26},{... | collective-permute-start | bytes 6291464 | tf_op jit(solution)/shard_map/ppermute | solution.py:34
  60.8 40.1 %collective-permute-done.8 = f32[8,64,1024]{2,1,0:T(8,128)S(1)} collective-permute-done((f32[8,64,1024]{2,1,0:T(8,128)S(1)}, f32[8,64,1024]{2,1,0:T(8,128)S(1)}, u32[]{:S(2)}, u32[]{:S(2)}) %collective-permute-start.8) | collective-permute-done | bytes 2097184 | tf_op jit(solution)/shard_map/ppermute | solution.py:34
  102.3 4.5 %collective-permute-start.9 = (f32[8,1,1024]{2,1,0:T(1,128)S(1)}, f32[8,1,1024]{2,1,0:T(1,128)S(1)}, u32[]{:S(2)}, u32[]{:S(2)}) collective-permute-start(f32[8,1,1024]{2,1,0:T(1,128)S(1)} %get-tuple-element.13), channel_id=1, source_target_pairs={{0,2},{2,4},{4,6},{1,3},{3,5},{5,7},{8,10},{10,12},{12,14},{9,11},... | collective-permute-start | bytes 98312 | tf_op jit(solution)/shard_map/ppermute | solution.py:22
  110.4 4.7 %collective-permute-start.11 = (f32[8,64,1024]{2,1,0:T(8,128)S(1)}, f32[8,64,1024]{2,1,0:T(8,128)S(1)}, u32[]{:S(2)}, u32[]{:S(2)}) collective-permute-start(f32[8,64,1024]{2,1,0:T(8,128)S(1)} %multiply_add_fusion.6), channel_id=1, source_target_pairs={{0,8},{8,16},{16,24},{1,9},{9,17},{17,25},{2,10},{10,18},{18,26},{... | collective-permute-start | bytes 6291464 | tf_op jit(solution)/shard_map/ppermute | solution.py:34
  115.1 37.9 %collective-permute-done.11 = f32[8,64,1024]{2,1,0:T(8,128)S(1)} collective-permute-done((f32[8,64,1024]{2,1,0:T(8,128)S(1)}, f32[8,64,1024]{2,1,0:T(8,128)S(1)}, u32[]{:S(2)}, u32[]{:S(2)}) %collective-permute-start.11) | collective-permute-done | bytes 2097184 | tf_op jit(solution)/shard_map/ppermute | solution.py:34
  153.0 3.9 %collective-permute-start.12 = (f32[8,1,1024]{2,1,0:T(1,128)S(1)}, f32[8,1,1024]{2,1,0:T(1,128)S(1)}, u32[]{:S(2)}, u32[]{:S(2)}) collective-permute-start(f32[8,1,1024]{2,1,0:T(1,128)S(1)} %get-tuple-element.9), channel_id=1, source_target_pairs={{0,2},{2,4},{4,6},{1,3},{3,5},{5,7},{8,10},{10,12},{12,14},{9,11},... | collective-permute-start | bytes 98312 | tf_op jit(solution)/shard_map/ppermute | solution.py:22
  159.1 3.7 %collective-permute-done.13 = f32[8,1,1024]{2,1,0:T(1,128)S(1)} collective-permute-done((f32[8,1,1024]{2,1,0:T(1,128)S(1)}, f32[8,1,1024]{2,1,0:T(1,128)S(1)}, u32[]{:S(2)}, u32[]{:S(2)}) %collective-permute-start.13) | collective-permute-done | bytes 32800 | tf_op jit(solution)/shard_map/ppermute | solution.py:24
  165.8 4.5 %collective-permute-start.14 = (f32[8,64,1024]{2,1,0:T(8,128)}, f32[8,64,1024]{2,1,0:T(8,128)S(1)}, u32[]{:S(2)}, u32[]{:S(2)}) collective-permute-start(f32[8,64,1024]{2,1,0:T(8,128)} %multiply_add_fusion.5), channel_id=1, source_target_pairs={{0,8},{8,16},{16,24},{1,9},{9,17},{17,25},{2,10},{10,18},{18,26},{... | collective-permute-start | bytes 6291464 | tf_op jit(solution)/shard_map/ppermute | solution.py:34
  172.2 33.8 %collective-permute-done.14 = f32[8,64,1024]{2,1,0:T(8,128)S(1)} collective-permute-done((f32[8,64,1024]{2,1,0:T(8,128)}, f32[8,64,1024]{2,1,0:T(8,128)S(1)}, u32[]{:S(2)}, u32[]{:S(2)}) %collective-permute-start.14) | collective-permute-done | bytes 2097184 | tf_op jit(solution)/shard_map/ppermute | solution.py:34
  206.0 3.1 collective-permute-start.15
  211.3 3.7 %collective-permute-done.16 = f32[8,1,1024]{2,1,0:T(1,128)S(1)} collective-permute-done((f32[8,1,1024]{2,1,0:T(1,128)S(1)}, f32[8,1,1024]{2,1,0:T(1,128)S(1)}, u32[]{:S(2)}, u32[]{:S(2)}) %collective-permute-start.16) | collective-permute-done | bytes 32800 | tf_op jit(solution)/shard_map/ppermute | solution.py:24
  218.0 17.9 %copy.18 = f32[8,64,1024]{0,2,1:T(8,128)} copy(f32[8,64,1024]{2,1,0:T(8,128)} %multiply_add_fusion.4) | data formatting | bytes 4194304 | tf_op jit(solution)/shard_map/add | solution.py:94
  235.9 11.1 %gather_fusion = f32[64,8]{1,0:T(8,128)S(1)} fusion(f32[8,65536]{0,1:T(8,128)} %bitcast.43, s32[1024]{0:T(1024)S(1)} %pad_clamp_fusion), kind=kCustom, calls=%fused_computation | custom fusion | bytes 4352 | tf_op jit(solution)/shard_map/jit(_take)/gather | solution.py:98
  249.3 74.4 %all-reduce.14 = (f32[16,16]{1,0:T(8,128)S(1)}, f32[16,16]{1,0:T(8,128)S(1)}) all-reduce(f32[16,16]{1,0:T(8,128)S(1)} %fusion.21, f32[16,16]{1,0:T(8,128)S(1)} %fusion.29), channel_id=1, replica_groups=mesh['tm'=4,'space'=4,'ens'=2] {'tm','space'}, use_global_device_ids=true, to_apply=%region_4.5 | all-reduce | flops 512 | bytes 4096 | tf_op jit(solution)/shard_map/psum | solution.py:111
  (90 shorter events, 40.2 us)
Async XLA Ops:
  1.7 13.8 %collective-permute-start = (f32[8,1,1024]{2,1,0:T(1,128)S(1)}, f32[8,1,1024]{2,1,0:T(1,128)S(1)}, u32[]{:S(2)}, u32[]{:S(2)}) collective-permute-start(f32[8,1,1024]{2,1,0:T(1,128)S(1)} %get-tuple-element.31), channel_id=1, source_target_pairs={{0,2},{2,4},{4,6},{1,3},{3,5},{5,7},{8,10},{10,12},{12,14},{9,11},... | collective-permute-start | bytes 98312 | tf_op jit(solution)/shard_map/ppermute | solution.py:22
  6.6 8.9 %collective-permute-start.1 = (f32[8,1,1024]{2,1,0:T(1,128)S(1)}, f32[8,1,1024]{2,1,0:T(1,128)S(1)}, u32[]{:S(2)}, u32[]{:S(2)}) collective-permute-start(f32[8,1,1024]{2,1,0:T(1,128)S(1)} %get-tuple-element.30), channel_id=1, source_target_pairs={{2,0},{4,2},{6,4},{3,1},{5,3},{7,5},{10,8},{12,10},{14,12},{11,9},... | collective-permute-start | bytes 98312 | tf_op jit(solution)/shard_map/ppermute | solution.py:24
  8.0 7.6 %copy-start = (f32[1,8,64,1024]{3,2,1,0:T(8,128)S(1)}, f32[1,8,64,1024]{3,2,1,0:T(8,128)}, u32[]{:S(2)}) copy-start(f32[1,8,64,1024]{3,2,1,0:T(8,128)} %param.10) | copy-start | bytes 6291460
  8.0 7.6 %copy-start.5 = (f32[64,1024]{1,0:T(8,128)S(1)}, f32[64,1024]{1,0:T(8,128)}, u32[]{:S(2)}) copy-start(f32[64,1024]{1,0:T(8,128)} %param.12) | copy-start | bytes 786436
  19.1 6.7 %collective-permute-start.2 = (f32[8,1,1024]{2,1,0:T(1,128)S(1)}, f32[8,1,1024]{2,1,0:T(1,128)S(1)}, u32[]{:S(2)}, u32[]{:S(2)}) collective-permute-start(f32[8,1,1024]{2,1,0:T(1,128)S(1)} %get-tuple-element.25), channel_id=1, source_target_pairs={{0,2},{2,4},{4,6},{1,3},{3,5},{5,7},{8,10},{10,12},{12,14},{9,11},... | collective-permute-start | bytes 98312 | tf_op jit(solution)/shard_map/ppermute | solution.py:22
  23.6 5.8 %collective-permute-start.3 = (f32[8,1,1024]{2,1,0:T(1,128)S(1)}, f32[8,1,1024]{2,1,0:T(1,128)S(1)}, u32[]{:S(2)}, u32[]{:S(2)}) collective-permute-start(f32[8,1,1024]{2,1,0:T(1,128)S(1)} %get-tuple-element.24), channel_id=1, source_target_pairs={{2,0},{4,2},{6,4},{3,1},{5,3},{7,5},{10,8},{12,10},{14,12},{11,9},... | collective-permute-start | bytes 98312 | tf_op jit(solution)/shard_map/ppermute | solution.py:24
  31.6 5.6 %collective-permute-start.4 = (f32[8,1,1024]{2,1,0:T(1,128)S(1)}, f32[8,1,1024]{2,1,0:T(1,128)S(1)}, u32[]{:S(2)}, u32[]{:S(2)}) collective-permute-start(f32[8,1,1024]{2,1,0:T(1,128)S(1)} %get-tuple-element.21), channel_id=1, source_target_pairs={{0,2},{2,4},{4,6},{1,3},{3,5},{5,7},{8,10},{10,12},{12,14},{9,11},... | collective-permute-start | bytes 98312 | tf_op jit(solution)/shard_map/ppermute | solution.py:22
  35.1 5.8 %collective-permute-start.5 = (f32[8,1,1024]{2,1,0:T(1,128)S(1)}, f32[8,1,1024]{2,1,0:T(1,128)S(1)}, u32[]{:S(2)}, u32[]{:S(2)}) collective-permute-start(f32[8,1,1024]{2,1,0:T(1,128)S(1)} %get-tuple-element.20), channel_id=1, source_target_pairs={{2,0},{4,2},{6,4},{3,1},{5,3},{7,5},{10,8},{12,10},{14,12},{11,9},... | collective-permute-start | bytes 98312 | tf_op jit(solution)/shard_map/ppermute | solution.py:24
  43.0 5.9 %collective-permute-start.6 = (f32[8,1,1024]{2,1,0:T(1,128)S(1)}, f32[8,1,1024]{2,1,0:T(1,128)S(1)}, u32[]{:S(2)}, u32[]{:S(2)}) collective-permute-start(f32[8,1,1024]{2,1,0:T(1,128)S(1)} %get-tuple-element.17), channel_id=1, source_target_pairs={{0,2},{2,4},{4,6},{1,3},{3,5},{5,7},{8,10},{10,12},{12,14},{9,11},... | collective-permute-start | bytes 98312 | tf_op jit(solution)/shard_map/ppermute | solution.py:22
  46.5 6.1 %collective-permute-start.7 = (f32[8,1,1024]{2,1,0:T(1,128)S(1)}, f32[8,1,1024]{2,1,0:T(1,128)S(1)}, u32[]{:S(2)}, u32[]{:S(2)}) collective-permute-start(f32[8,1,1024]{2,1,0:T(1,128)S(1)} %get-tuple-element.16), channel_id=1, source_target_pairs={{2,0},{4,2},{6,4},{3,1},{5,3},{7,5},{10,8},{12,10},{14,12},{11,9},... | collective-permute-start | bytes 98312 | tf_op jit(solution)/shard_map/ppermute | solution.py:24
  57.3 105.5 %copy-start.1 = (f32[8,64,1024]{2,1,0:T(8,128)}, f32[8,64,1024]{2,1,0:T(8,128)S(1)}, u32[]{:S(2)}) copy-start(f32[8,64,1024]{2,1,0:T(8,128)S(1)} %subtract_select_fusion) | copy-start | bytes 6291460
  57.3 43.6 %collective-permute-start.8 = (f32[8,64,1024]{2,1,0:T(8,128)S(1)}, f32[8,64,1024]{2,1,0:T(8,128)S(1)}, u32[]{:S(2)}, u32[]{:S(2)}) collective-permute-start(f32[8,64,1024]{2,1,0:T(8,128)S(1)} %subtract_select_fusion), channel_id=1, source_target_pairs={{0,8},{8,16},{16,24},{1,9},{9,17},{17,25},{2,10},{10,18},{18,26},{... | collective-permute-start | bytes 6291464 | tf_op jit(solution)/shard_map/ppermute | solution.py:34
  101.0 6.7 %collective-permute-start.10 = (f32[8,1,1024]{2,1,0:T(1,128)S(1)}, f32[8,1,1024]{2,1,0:T(1,128)S(1)}, u32[]{:S(2)}, u32[]{:S(2)}) collective-permute-start(f32[8,1,1024]{2,1,0:T(1,128)S(1)} %get-tuple-element.12), channel_id=1, source_target_pairs={{2,0},{4,2},{6,4},{3,1},{5,3},{7,5},{10,8},{12,10},{14,12},{11,9},... | collective-permute-start | bytes 98312 | tf_op jit(solution)/shard_map/ppermute | solution.py:24
  102.3 6.1 %collective-permute-start.9 = (f32[8,1,1024]{2,1,0:T(1,128)S(1)}, f32[8,1,1024]{2,1,0:T(1,128)S(1)}, u32[]{:S(2)}, u32[]{:S(2)}) collective-permute-start(f32[8,1,1024]{2,1,0:T(1,128)S(1)} %get-tuple-element.13), channel_id=1, source_target_pairs={{0,2},{2,4},{4,6},{1,3},{3,5},{5,7},{8,10},{10,12},{12,14},{9,11},... | collective-permute-start | bytes 98312 | tf_op jit(solution)/shard_map/ppermute | solution.py:22
  110.4 42.6 %collective-permute-start.11 = (f32[8,64,1024]{2,1,0:T(8,128)S(1)}, f32[8,64,1024]{2,1,0:T(8,128)S(1)}, u32[]{:S(2)}, u32[]{:S(2)}) collective-permute-start(f32[8,64,1024]{2,1,0:T(8,128)S(1)} %multiply_add_fusion.6), channel_id=1, source_target_pairs={{0,8},{8,16},{16,24},{1,9},{9,17},{17,25},{2,10},{10,18},{18,26},{... | collective-permute-start | bytes 6291464 | tf_op jit(solution)/shard_map/ppermute | solution.py:34
  153.0 6.1 %collective-permute-start.12 = (f32[8,1,1024]{2,1,0:T(1,128)S(1)}, f32[8,1,1024]{2,1,0:T(1,128)S(1)}, u32[]{:S(2)}, u32[]{:S(2)}) collective-permute-start(f32[8,1,1024]{2,1,0:T(1,128)S(1)} %get-tuple-element.9), channel_id=1, source_target_pairs={{0,2},{2,4},{4,6},{1,3},{3,5},{5,7},{8,10},{10,12},{12,14},{9,11},... | collective-permute-start | bytes 98312 | tf_op jit(solution)/shard_map/ppermute | solution.py:22
  157.0 5.8 %collective-permute-start.13 = (f32[8,1,1024]{2,1,0:T(1,128)S(1)}, f32[8,1,1024]{2,1,0:T(1,128)S(1)}, u32[]{:S(2)}, u32[]{:S(2)}) collective-permute-start(f32[8,1,1024]{2,1,0:T(1,128)S(1)} %get-tuple-element.8), channel_id=1, source_target_pairs={{2,0},{4,2},{6,4},{3,1},{5,3},{7,5},{10,8},{12,10},{14,12},{11,9},... | collective-permute-start | bytes 98312 | tf_op jit(solution)/shard_map/ppermute | solution.py:24
  162.8 9.3 %copy-start.12 = (s32[1,64]{1,0:T(1,128)S(1)}, s32[1,64]{1,0:T(1,128)}, u32[]{:S(2)}) copy-start(s32[1,64]{1,0:T(1,128)} %param.16) | copy-start | bytes 772
  162.8 9.4 %copy-start.13 = (f32[1,64]{1,0:T(1,128)S(1)}, f32[1,64]{1,0:T(1,128)}, u32[]{:S(2)}) copy-start(f32[1,64]{1,0:T(1,128)} %param.19) | copy-start | bytes 772
  165.8 40.2 %collective-permute-start.14 = (f32[8,64,1024]{2,1,0:T(8,128)}, f32[8,64,1024]{2,1,0:T(8,128)S(1)}, u32[]{:S(2)}, u32[]{:S(2)}) collective-permute-start(f32[8,64,1024]{2,1,0:T(8,128)} %multiply_add_fusion.5), channel_id=1, source_target_pairs={{0,8},{8,16},{16,24},{1,9},{9,17},{17,25},{2,10},{10,18},{18,26},{... | collective-permute-start | bytes 6291464 | tf_op jit(solution)/shard_map/ppermute | solution.py:34
  206.0 5.3 %collective-permute-start.15 = (f32[8,1,1024]{2,1,0:T(1,128)S(1)}, f32[8,1,1024]{2,1,0:T(1,128)S(1)}, u32[]{:S(2)}, u32[]{:S(2)}) collective-permute-start(f32[8,1,1024]{2,1,0:T(1,128)S(1)} %get-tuple-element.5), channel_id=1, source_target_pairs={{0,2},{2,4},{4,6},{1,3},{3,5},{5,7},{8,10},{10,12},{12,14},{9,11},... | collective-permute-start | bytes 98312 | tf_op jit(solution)/shard_map/ppermute | solution.py:22
  209.1 5.9 %collective-permute-start.16 = (f32[8,1,1024]{2,1,0:T(1,128)S(1)}, f32[8,1,1024]{2,1,0:T(1,128)S(1)}, u32[]{:S(2)}, u32[]{:S(2)}) collective-permute-start(f32[8,1,1024]{2,1,0:T(1,128)S(1)} %get-tuple-element.4), channel_id=1, source_target_pairs={{2,0},{4,2},{6,4},{3,1},{5,3},{7,5},{10,8},{12,10},{14,12},{11,9},... | collective-permute-start | bytes 98312 | tf_op jit(solution)/shard_map/ppermute | solution.py:24
  218.0 31.1 %copy-start.10 = (f32[1,64,16]{1,2,0:T(8,128)S(1)}, f32[1,64,16]{1,2,0:T(8,128)}, u32[]{:S(2)}) copy-start(f32[1,64,16]{1,2,0:T(8,128)} %param.18) | copy-start | bytes 12292
  218.0 31.1 %copy-start.11 = (f32[1,64]{1,0:T(1,128)S(1)}, f32[1,64]{1,0:T(1,128)}, u32[]{:S(2)}) copy-start(f32[1,64]{1,0:T(1,128)} %param.17) | copy-start | bytes 772
  (7 other events, 46.0 us)
where the time goes:
time: 330 us; the launch traced here: 329 us
  waiting for transfers between devices  131 us (40%)
  blocking collectives  78 us (24%)
  starting transfers between devices  50.2 us (15%)
  local copies, waits for them, and re-layouts  43 us (13%)
  other arithmetic  24.3 us (7%)
    ppermute x3, waiting for transfers between devices, shifted(): lax.ppermute(value, axis, [(source, source + steps) for source in range(f...  112 us
    psum x1, blocking collectives, per_device(): gram, cross = lax.psum((gram, cross), ('tm', 'space'))  74.4 us
    ppermute x7, starting transfers between devices, with_halo(): lax.ppermute(tail, axis, [(i, (i + 1) % count) for i in range(ends)])  28 us
    ppermute x7, waiting for transfers between devices, with_halo(): lax.ppermute(head, axis, [((i + 1) % count, i) for i in range(ends)])  18.4 us
    add x1, local copies, waits for them, and re-layouts, per_device(): running = correction + advance(padded, coeffs, own_rows, coarse_dt, None)  17.9 us
    ppermute x3, starting transfers between devices, shifted(): lax.ppermute(value, axis, [(source, source + steps) for source in range(f...  12.7 us
    gather x1, local copies, waits for them, and re-layouts, per_device(): predicted = jnp.take(flat, local_cell, axis=1)  11.1 us
    slice x7, local copies, waits for them, and re-layouts, advance(): west_cell = jnp.pad(middle[:, :, :-1], ((0, 0), (0, 0), (1, 0)))  10.1 us
  transfers between devices with their start and end apart: 17, of which 9 were waited for; matrix products, arithmetic and copies ran while one was open for 4% of the time, Pallas kernels for 0%

commit v1 on v0

v1 whole, which is shorter than its diff:
```python
import functools
import math

import jax
import jax.numpy as jnp
from jax import lax
from jax.experimental import pallas as pl
from jax.experimental.pallas import tpu as pltpu
from jax.sharding import PartitionSpec as P

FINE = 4
FINE_DT = 0.25
PAD = 8
MESH = pl.DeviceIdType.MESH
HIGH = lax.Precision.HIGHEST
NT = (((1,), (1,)), ((), ()))
TN = (((0,), (0,)), ((), ()))


def kernel(
    sizes,
    start_ref, vx_ref, vy_ref, diff_ref, src_ref, params_ref,
    cell_ref, data_ref, noise_ref, var_ref,
    out_ref, new_params_ref,
    st, a1, a2, a3, nw, rv, craw, cf, par, pall, xall, gtm, gsp,
    halo_send, halo_recv, row_send, row_recv, edge_send, edge_recv,
    ens_send, ens_recv, tm_send, tm_recv, sp_send, sp_recv,
):
    n_tm, n_sp, n_ens = sizes
    me_tm = lax.axis_index("tm")
    me_sp = lax.axis_index("space")
    me_ens = lax.axis_index("ens")
    members, rows, cols = start_ref.shape
    half = rows // 2
    bands = params_ref.shape[1]
    n_obs = data_ref.shape[1]
    other = 1 - me_ens
    first, last = me_sp == 0, me_sp == n_sp - 1
    up_sp = lax.rem(me_sp + n_sp - 1, n_sp)
    dn_sp = lax.rem(me_sp + 1, n_sp)
    next_tm = lax.rem(me_tm + 1, n_tm)
    prev_tm = lax.rem(me_tm + n_tm - 1, n_tm)

    barrier = pltpu.get_barrier_semaphore()
    greeted = [{"ens": other}]
    greeted += [{"tm": lax.rem(me_tm + k, n_tm)} for k in range(1, n_tm)]
    greeted += [{"space": lax.rem(me_sp + k, n_sp)} for k in range(1, n_sp)]
    greeted += [{"tm": t, "space": s} for t in (next_tm, prev_tm) for s in (up_sp, dn_sp)]
    for device in greeted:
        pl.semaphore_signal(barrier, inc=1, device_id=device, device_id_type=MESH)

    for k, ref in enumerate((diff_ref, vx_ref, vy_ref, src_ref)):
        craw[k, PAD:PAD + rows, :] = ref[...]

    @pl.loop(0, rows // 8)
    def _(k):
        at = pl.multiple_of(k * 8, 8)
        st[pl.ds(PAD + at, 8)] = jnp.swapaxes(start_ref[:, pl.ds(at, 8), :], 0, 1)

    pl.semaphore_wait(barrier, len(greeted))

    def remote(src, dst, send, recv, device):
        return pltpu.make_async_remote_copy(
            src_ref=src, dst_ref=dst, send_sem=send, recv_sem=recv,
            device_id=device, device_id_type=MESH,
        )

    up = {"space": up_sp}
    down = {"space": dn_sp}
    coef_up = remote(craw.at[:, pl.ds(PAD, 8)], craw.at[:, pl.ds(PAD + rows, 8)],
                     halo_send.at[0], halo_recv.at[0], up)
    coef_down = remote(craw.at[:, pl.ds(PAD + rows - 8, 8)], craw.at[:, pl.ds(0, 8)],
                       halo_send.at[1], halo_recv.at[1], down)
    state_up = remote(st.at[pl.ds(PAD, FINE)], st.at[pl.ds(PAD + rows, FINE)],
                      halo_send.at[2], halo_recv.at[2], up)
    state_down = remote(st.at[pl.ds(PAD + rows - FINE, FINE)], st.at[pl.ds(PAD - FINE, FINE)],
                        halo_send.at[3], halo_recv.at[3], down)

    @pl.when(jnp.logical_not(first))
    def _():
        coef_up.start()
        state_up.start()

    @pl.when(jnp.logical_not(last))
    def _():
        coef_down.start()
        state_down.start()

    share_params = remote(params_ref, pall.at[me_ens], ens_send.at[0], ens_recv.at[0], {"ens": other})
    share_params.start()
    pall[me_ens] = params_ref[...]

    @pl.when(first)
    def _():
        craw[:, 0:PAD, :] = jnp.zeros((4, PAD, cols), jnp.float32)
        st[0:PAD] = jnp.zeros((PAD, members, cols), jnp.float32)
        rv[0] = jnp.zeros((members, cols), jnp.float32)

    @pl.when(last)
    def _():
        craw[:, PAD + rows:, :] = jnp.zeros((4, PAD, cols), jnp.float32)
        st[PAD + rows:] = jnp.zeros((PAD, members, cols), jnp.float32)
        rv[rows + 1] = jnp.zeros((members, cols), jnp.float32)

    pick = (lax.broadcasted_iota(jnp.int32, (bands, cols), 1) // (cols // bands)
            == lax.broadcasted_iota(jnp.int32, (bands, cols), 0)).astype(jnp.float32)
    par[...] = jnp.dot(params_ref[...], pick, precision=HIGH, preferred_element_type=jnp.float32)

    mine = (lax.broadcasted_iota(jnp.int32, (members, members * n_ens), 1)
            == lax.broadcasted_iota(jnp.int32, (members, members * n_ens), 0) + me_ens * members)
    noise = lax.dot_general(mine.astype(jnp.float32), noise_ref[0], NT, precision=HIGH,
                            preferred_element_type=jnp.float32)
    target = data_ref[...] + noise
    inv_spread = lax.rsqrt(var_ref[...])

    @pl.when(jnp.logical_not(last))
    def _():
        coef_up.wait_recv()
        state_up.wait_recv()

    @pl.when(jnp.logical_not(first))
    def _():
        coef_down.wait_recv()
        state_down.wait_recv()

    lane = lax.broadcasted_iota(jnp.int32, (8, cols), 1)

    @pl.loop(0, (rows + 2 * PAD) // 8)
    def _(k):
        at = pl.ds(pl.multiple_of(k * 8, 8), 8)
        d = craw[0, at, :] * FINE_DT
        hx = craw[1, at, :] * (0.5 * FINE_DT)
        hy = craw[2, at, :] * (0.5 * FINE_DT)
        parts = [
            -4.0 * d, d + hy, d - hy,
            jnp.where(lane == 0, 0.0, d + hx),
            jnp.where(lane == cols - 1, 0.0, d - hx),
            craw[3, at, :] * FINE_DT, d, d,
        ]
        cf[at] = jnp.swapaxes(jnp.stack(parts, axis=0), 0, 1)

    def spread(row, above, middle, below):
        c = [cf[row + PAD, k:k + 1, :] for k in range(5)]
        return (c[0] * middle + c[1] * above + c[2] * below
                + c[3] * pltpu.roll(middle, 1, 1) + c[4] * pltpu.roll(middle, cols - 1, 1))

    def fine(field, row):
        at = row + PAD
        middle = field[at]
        force = cf[at, 5:6, :] * par[...]
        return middle + (spread(row, field[at - 1], middle, field[at + 1]) + force)

    def row_copy(row):
        return remote(nw.at[row], rv.at[row + 1], row_send.at[row], row_recv.at[row], {"tm": next_tm})

    edge_up = remote(nw.at[0], rv.at[rows + 1], edge_send.at[0], edge_recv.at[0],
                     {"tm": next_tm, "space": up_sp})
    edge_down = remote(nw.at[rows - 1], rv.at[0], edge_send.at[1], edge_recv.at[1],
                       {"tm": next_tm, "space": dn_sp})
    sends = me_tm < n_tm - 1
    receives = me_tm > 0

    def coarse(row):
        above, middle, below = (rv[row + k] - st[row + PAD - 1 + k] for k in range(3))
        return middle + spread(row, above, middle, below) * float(FINE)

    @pl.loop(0, half + 6)
    def _(step):
        t = step - 3
        for top in (True, False):
            def place(r):
                return r if top else rows - 1 - r
            a1[place(t) + PAD] = fine(st, place(t))
            a2[place(t - 1) + PAD] = fine(a1, place(t - 1))
            a3[place(t - 2) + PAD] = fine(a2, place(t - 2))
        q = t - 3

        @pl.when(q >= 0)
        def _():
            nw[q] = fine(a3, q)
            nw[rows - 1 - q] = fine(a3, rows - 1 - q)

            @pl.when(receives)
            def _():
                @pl.when(q == 0)
                def _():
                    row_copy(0).wait_recv()
                    row_copy(rows - 1).wait_recv()

                    @pl.when(jnp.logical_not(last))
                    def _():
                        edge_up.wait_recv()

                    @pl.when(jnp.logical_not(first))
                    def _():
                        edge_down.wait_recv()

                @pl.when(q < half - 1)
                def _():
                    row_copy(q + 1).wait_recv()
                    row_copy(rows - 2 - q).wait_recv()

                nw[q] = nw[q] + coarse(q)
                nw[rows - 1 - q] = nw[rows - 1 - q] + coarse(rows - 1 - q)

            @pl.when(sends)
            def _():
                @pl.when(q == 0)
                def _():
                    @pl.when(jnp.logical_not(first))
                    def _():
                        edge_up.start()

                    @pl.when(jnp.logical_not(last))
                    def _():
                        edge_down.start()

                row_copy(q).start()
                row_copy(rows - 1 - q).start()

    lanes = lax.broadcasted_iota(jnp.int32, (members, 128), 1)
    wide = lax.broadcasted_iota(jnp.int32, (members, cols), 1)

    def gather(o, found):
        cell = lax.rem(cell_ref[0, o], rows * cols)
        row = lax.div(cell, cols)
        col = lax.rem(cell, cols)
        value = jnp.sum(jnp.where(wide == col, nw[row], 0.0), axis=1, keepdims=True)
        return jnp.where(lanes == o, value, found)

    found = lax.fori_loop(0, n_obs, gather, jnp.zeros((members, 128), jnp.float32), unroll=8)
    predicted = found[:, :n_obs]
    xall[me_ens] = jnp.concatenate(
        [predicted * inv_spread, (target - predicted) * inv_spread], axis=1)
    share_pred = remote(xall.at[me_ens], xall.at[me_ens], ens_send.at[1], ens_recv.at[1], {"ens": other})
    share_pred.start()

    @pl.loop(0, rows // 8)
    def _(k):
        at = pl.multiple_of(k * 8, 8)
        out_ref[:, pl.ds(at, 8), :] = jnp.swapaxes(nw[pl.ds(at, 8)], 0, 1)

    share_pred.wait()
    total = members * n_ens
    norm_factor = 1.0 / math.sqrt(total - 1)
    everyone = jnp.concatenate([xall[e] for e in range(n_ens)], axis=0)
    scaled, misfit = everyone[:, :n_obs], everyone[:, n_obs:]
    anomaly = (scaled - jnp.mean(scaled, axis=0, keepdims=True)) * norm_factor
    right = jnp.concatenate(
        [anomaly, misfit, jnp.zeros((128 - 2 * total, n_obs), jnp.float32)], axis=0)
    gtm[me_tm] = lax.dot_general(anomaly, right, NT, precision=HIGH,
                                 preferred_element_type=jnp.float32)

    def add_up(buffer, axis, me, count, send, recv):
        peers = [lax.rem(me + k, count) for k in range(1, count)]
        for peer in peers:
            remote(buffer.at[me], buffer.at[me], send.at[peer], recv.at[me], {axis: peer}).start()
        for peer in peers:
            remote(buffer.at[peer], buffer.at[peer], send.at[peer], recv.at[peer], {axis: peer}).wait_recv()
        summed = buffer[0]
        for k in range(1, count):
            summed = summed + buffer[k]
        return summed, peers

    summed, tm_peers = add_up(gtm, "tm", me_tm, n_tm, tm_send, tm_recv)
    gsp[me_sp] = summed
    system, sp_peers = add_up(gsp, "space", me_sp, n_sp, sp_send, sp_recv)

    row_no = lax.broadcasted_iota(jnp.int32, (total, 128), 0)
    system = system + (row_no == lax.broadcasted_iota(jnp.int32, (total, 128), 1)).astype(jnp.float32)
    for k in range(total):
        pivot_row = system[k:k + 1, :] / system[k:k + 1, k:k + 1]
        system = jnp.where(row_no == k, pivot_row, system - system[:, k:k + 1] * pivot_row)
    weights = system[:, total:2 * total]

    share_params.wait()
    every_param = jnp.concatenate([pall[e] for e in range(n_ens)], axis=0)
    param_anom = every_param - jnp.mean(every_param, axis=0, keepdims=True)
    update = lax.dot_general(weights, param_anom, TN, precision=HIGH,
                             preferred_element_type=jnp.float32) * norm_factor
    own = jnp.where(me_ens == 0, update[:members], update[members:])
    new_params_ref[...] = params_ref[...] + own

    @pl.when(jnp.logical_not(first))
    def _():
        coef_up.wait_send()
        state_up.wait_send()

    @pl.when(jnp.logical_not(last))
    def _():
        coef_down.wait_send()
        state_down.wait_send()

    @pl.when(sends)
    def _():
        @pl.when(jnp.logical_not(first))
        def _():
            edge_up.wait_send()

        @pl.when(jnp.logical_not(last))
        def _():
            edge_down.wait_send()

        @pl.loop(0, rows)
        def _(row):
            row_copy(row).wait_send()

    for peer in tm_peers:
        remote(gtm.at[me_tm], gtm.at[me_tm], tm_send.at[peer], tm_recv.at[me_tm], {"tm": peer}).wait_send()
    for peer in sp_peers:
        remote(gsp.at[me_sp], gsp.at[me_sp], sp_send.at[peer], sp_recv.at[me_sp], {"space": peer}).wait_send()


def per_device(sizes, start_states, velocity_x, velocity_y, diffusivity, source_shape, params,
               obs_cell, obs_data, obs_noise, obs_var):
    state = start_states[0]
    members, rows, cols = state.shape
    n_tm, n_sp, n_ens = sizes
    total = members * n_ens
    padded = (rows + 2 * PAD, members, cols)
    f32 = jnp.float32
    vmem = pl.BlockSpec(memory_space=pltpu.VMEM)
    dma = pltpu.SemaphoreType.DMA
    new_states, new_params = pl.pallas_call(
        functools.partial(kernel, sizes),
        out_shape=(jax.ShapeDtypeStruct(state.shape, f32), jax.ShapeDtypeStruct(params.shape, f32)),
        in_specs=[vmem] * 6 + [pl.BlockSpec(memory_space=pltpu.SMEM)] + [vmem] * 3,
        out_specs=(vmem, vmem),
        scratch_shapes=[
            pltpu.VMEM(padded, f32),
            pltpu.VMEM(padded, f32),
            pltpu.VMEM(padded, f32),
            pltpu.VMEM(padded, f32),
            pltpu.VMEM((rows, members, cols), f32),
            pltpu.VMEM((rows + 2, members, cols), f32),
            pltpu.VMEM((4, rows + 2 * PAD, cols), f32),
            pltpu.VMEM((rows + 2 * PAD, 8, cols), f32),
            pltpu.VMEM((members, cols), f32),
            pltpu.VMEM((n_ens,) + params.shape, f32),
            pltpu.VMEM((n_ens, members, 128), f32),
            pltpu.VMEM((n_tm, total, 128), f32),
            pltpu.VMEM((n_sp, total, 128), f32),
            dma((4,)), dma((4,)),
            dma((rows,)), dma((rows,)),
            dma((2,)), dma((2,)),
            dma((2,)), dma((2,)),
            dma((n_tm,)), dma((n_tm,)),
            dma((n_sp,)), dma((n_sp,)),
        ],
        compiler_params=pltpu.CompilerParams(
            collective_id=0, has_side_effects=True, vmem_limit_bytes=48 * 2**20
        ),
    )(state, velocity_x, velocity_y, diffusivity, source_shape, params,
      obs_cell, obs_data, obs_noise, obs_var)
    return (new_states[None], new_params)


def solution(mesh):
    sizes = tuple(mesh.shape[axis] for axis in ("tm", "space", "ens"))
    in_specs = (
        P("tm", "ens", "space", None),
        P("space", None),
        P("space", None),
        P("space", None),
        P("space", None),
        P("ens", None),
        P("tm", "space"),
        P("tm", "space"),
        P("tm", "space", None),
        P("tm", "space"),
    )
    out_specs = (P("tm", "ens", "space", None), P("ens", None))
    return jax.shard_map(
        functools.partial(per_device, sizes), mesh=mesh,
        in_specs=in_specs, out_specs=out_specs, check_vma=False,
    )
```

time: 330 us -> 99.3 us (0.30)
  waiting for transfers between devices: 131 us -> 0 us
  Pallas kernels: 0 us -> 87.6 us
  blocking collectives: 78 us -> 0 us
  starting transfers between devices: 50.2 us -> 0 us
  local copies, waits for them, and re-layouts: 43 us -> 10.7 us
  other arithmetic: 24.3 us -> 0 us
    ppermute x17 -> x0, waiting for transfers between devices: 131 us -> none  [the longest x3 112 us: shifted(): lax.ppermute(value, axis, [(source, source + steps) for source in range(f...]
    pallas_call x0 -> x1, Pallas kernels: none -> 87.6 us  [per_device(): pl.pallas_call(functools.partial(kernel, sizes), out_shape=(jax.ShapeDtyp...]
    psum x1 -> x0, blocking collectives: 74.4 us -> none  [per_device(): gram, cross = lax.psum((gram, cross), ('tm', 'space'))]
    ppermute x17 -> x0, starting transfers between devices: 50.2 us -> none  [the longest x7 28 us: with_halo(): lax.ppermute(tail, axis, [(i, (i + 1) % count) for i in range(ends)])]
    add x2 -> x0, local copies, waits for them, and re-layouts: 18 us -> none  [the longest x1 17.9 us: per_device(): running = correction + advance(padded, coeffs, own_rows, coarse_dt, None)]
    slice x14 -> x0, local copies, waits for them, and re-layouts: 11.4 us -> none  [the longest x7 10.1 us: advance(): west_cell = jnp.pad(middle[:, :, :-1], ((0, 0), (0, 0), (1, 0)))]
    gather x1 -> x0, local copies, waits for them, and re-layouts: 11.1 us -> none  [per_device(): predicted = jnp.take(flat, local_cell, axis=1)]
    unnamed x28 -> x21, local copies, waits for them, and re-layouts: 0.08 us -> 10.7 us
  transfers between devices with their start and end apart: 17 -> 0, of which waited for: 9 -> 0; matrix products, arithmetic and copies ran while one was open for 4% -> 0% of each run, Pallas kernels for 0% -> 0%
where the time goes in v1:
time: 99.3 us; the launch traced here: 99 us
  Pallas kernels  87.6 us (88%)
  local copies, waits for them, and re-layouts  10.7 us (11%)
    pallas_call x1, Pallas kernels, per_device(): pl.pallas_call(functools.partial(kernel, sizes), out_shape=(jax.ShapeDtyp...  87.6 us
    unnamed x21, local copies, waits for them, and re-layouts  10.7 us

profile of v1, /device:TPU:0, one launch (start us, length us, event | category | flops | bytes accessed | tf_op | source)
XLA Modules:
  0.0 99.0 jit_solution(11126778575317288620)
XLA Ops:
  0.6 0.8 copy.12.noise_ref
  1.4 0.0 copy-start
  1.4 1.6 %copy-done = f32[1,8,64,1024]{3,2,1,0:T(8,128)S(1)} copy-done((f32[1,8,64,1024]{3,2,1,0:T(8,128)S(1)}, f32[1,8,64,1024]{3,2,1,0:T(8,128)}, u32[]{:S(2)}) %copy-start) | copy-done | bytes 2097176
  3.0 0.0 copy-start.1
  3.0 0.9 copy-done.1
  4.0 0.0 copy-start.2
  4.0 0.9 copy-done.2
  4.9 0.0 copy-start.3
  4.9 0.9 copy-done.3
  5.9 0.0 copy-start.4
  5.9 0.9 copy-done.4
  6.8 0.0 copy-start.5
  6.8 0.7 copy-done.5
  7.5 0.0 copy-start.6
  7.5 0.7 copy-done.6
  8.1 0.0 copy-start.7
  8.1 0.7 copy-done.7
  8.8 0.0 copy-start.8
  8.8 0.7 copy-done.8
  9.5 87.6 %shard_map.113 = (f32[8,64,1024]{2,1,0:T(8,128)S(1)}, f32[8,128]{1,0:T(8,128)S(1)}) custom-call(f32[8,64,1024]{2,1,0:T(8,128)S(1)} %bitcast.2, f32[64,1024]{1,0:T(8,128)S(1)} %copy-done.1, f32[64,1024]{1,0:T(8,128)S(1)} %copy-done.2, f32[64,1024]{1,0:T(8,128)S(1)} %copy-done.3, f32[64,1024]{1,0:T(8,128)S(1)} %copy-done.4, f32[8,128]{1,0:T(8,128)S(1)} %copy-done.5, ...), custom_call_target="tpu_custom_call" | custom-call | tf_op jit(solution)/shard_map/pallas_call | solution.py:324
  97.0 1.3 %copy.15 = f32[1,8,64,1024]{3,2,1,0:T(8,128)} copy(f32[1,8,64,1024]{3,2,1,0:T(8,128)S(1)} %bitcast.3) | data formatting | bytes 4194304
  98.4 0.6 copy.16
Async XLA Ops:
  1.4 1.6 %copy-start = (f32[1,8,64,1024]{3,2,1,0:T(8,128)S(1)}, f32[1,8,64,1024]{3,2,1,0:T(8,128)}, u32[]{:S(2)}) copy-start(f32[1,8,64,1024]{3,2,1,0:T(8,128)} %param.10) | copy-start | bytes 6291460
  3.0 0.9 copy-start.1
  4.0 0.9 copy-start.2
  4.9 0.9 copy-start.3
  5.9 0.9 copy-start.4
  6.8 0.7 copy-start.5
  7.5 0.7 copy-start.6
  8.1 0.7 copy-start.7
  8.8 0.7 copy-start.8

commit v2 on v1

--- a/solution.py
+++ b/solution.py
@@ -19,10 +19,12 @@
 
 def kernel(
     sizes,
-    start_ref, vx_ref, vy_ref, diff_ref, src_ref, params_ref,
-    cell_ref, data_ref, noise_ref, var_ref,
-    out_ref, new_params_ref,
+    start_hbm, vx_hbm, vy_hbm, diff_hbm, src_hbm, params_hbm,
+    cell_hbm, data_hbm, noise_hbm, var_hbm,
+    out_hbm, new_params_ref,
+    start_ref, out_ref, params_ref, cell_ref, data_ref, noise_ref, var_ref,
     st, a1, a2, a3, nw, rv, craw, cf, par, pall, xall, gtm, gsp,
+    in_sem, small_sem, block_sem, out_sem,
     halo_send, halo_recv, row_send, row_recv, edge_send, edge_recv,
     ens_send, ens_recv, tm_send, tm_recv, sp_send, sp_recv,
 ):
@@ -32,6 +34,7 @@
     me_ens = lax.axis_index("ens")
     members, rows, cols = start_ref.shape
     half = rows // 2
+    pairs = half // 8
     bands = params_ref.shape[1]
     n_obs = data_ref.shape[1]
     other = 1 - me_ens
@@ -40,6 +43,40 @@
     dn_sp = lax.rem(me_sp + 1, n_sp)
     next_tm = lax.rem(me_tm + 1, n_tm)
     prev_tm = lax.rem(me_tm + n_tm - 1, n_tm)
+    sends = me_tm < n_tm - 1
+    receives = me_tm > 0
+
+    def block_of(pair, side):
+        at = half - 8 - 8 * pair if side == 0 else half + 8 * pair
+        return at if isinstance(pair, int) else pl.multiple_of(at, 8)
+
+    def start_in(pair, side):
+        at = pl.ds(block_of(pair, side), 8)
+        return pltpu.make_async_copy(start_hbm.at[:, at], start_ref.at[:, at], block_sem.at[side, pair])
+
+    def coef_in(k):
+        ref = (diff_hbm, vx_hbm, vy_hbm, src_hbm)[k]
+        return pltpu.make_async_copy(ref, craw.at[k, pl.ds(PAD, rows)], in_sem.at[k])
+
+    def result_out(pair, side):
+        at = pl.ds(block_of(pair, side), 8)
+        return pltpu.make_async_copy(out_ref.at[:, at], out_hbm.at[:, at], out_sem.at[side, pair])
+
+    small = [
+        pltpu.make_async_copy(src, dst, small_sem.at[k])
+        for k, (src, dst) in enumerate((
+            (params_hbm, params_ref), (cell_hbm, cell_ref), (data_hbm, data_ref),
+            (noise_hbm, noise_ref), (var_hbm, var_ref)))
+    ]
+    start_in(0, 0).start()
+    start_in(0, 1).start()
+    for k in range(4):
+        coef_in(k).start()
+    for copy in small:
+        copy.start()
+    for pair in range(1, pairs):
+        start_in(pair, 0).start()
+        start_in(pair, 1).start()
 
     barrier = pltpu.get_barrier_semaphore()
     greeted = [{"ens": other}]
@@ -48,16 +85,6 @@
     greeted += [{"tm": t, "space": s} for t in (next_tm, prev_tm) for s in (up_sp, dn_sp)]
     for device in greeted:
         pl.semaphore_signal(barrier, inc=1, device_id=device, device_id_type=MESH)
-
-    for k, ref in enumerate((diff_ref, vx_ref, vy_ref, src_ref)):
-        craw[k, PAD:PAD + rows, :] = ref[...]
-
-    @pl.loop(0, rows // 8)
-    def _(k):
-        at = pl.multiple_of(k * 8, 8)
-        st[pl.ds(PAD + at, 8)] = jnp.swapaxes(start_ref[:, pl.ds(at, 8), :], 0, 1)
-
-    pl.semaphore_wait(barrier, len(greeted))
 
     def remote(src, dst, send, recv, device):
         return pltpu.make_async_remote_copy(
@@ -76,58 +103,10 @@
     state_down = remote(st.at[pl.ds(PAD + rows - FINE, FINE)], st.at[pl.ds(PAD - FINE, FINE)],
                         halo_send.at[3], halo_recv.at[3], down)
 
-    @pl.when(jnp.logical_not(first))
-    def _():
-        coef_up.start()
-        state_up.start()
-
-    @pl.when(jnp.logical_not(last))
-    def _():
-        coef_down.start()
-        state_down.start()
-
-    share_params = remote(params_ref, pall.at[me_ens], ens_send.at[0], ens_recv.at[0], {"ens": other})
-    share_params.start()
-    pall[me_ens] = params_ref[...]
-
-    @pl.when(first)
-    def _():
-        craw[:, 0:PAD, :] = jnp.zeros((4, PAD, cols), jnp.float32)
-        st[0:PAD] = jnp.zeros((PAD, members, cols), jnp.float32)
-        rv[0] = jnp.zeros((members, cols), jnp.float32)
-
-    @pl.when(last)
-    def _():
-        craw[:, PAD + rows:, :] = jnp.zeros((4, PAD, cols), jnp.float32)
-        st[PAD + rows:] = jnp.zeros((PAD, members, cols), jnp.float32)
-        rv[rows + 1] = jnp.zeros((members, cols), jnp.float32)
-
-    pick = (lax.broadcasted_iota(jnp.int32, (bands, cols), 1) // (cols // bands)
-            == lax.broadcasted_iota(jnp.int32, (bands, cols), 0)).astype(jnp.float32)
-    par[...] = jnp.dot(params_ref[...], pick, precision=HIGH, preferred_element_type=jnp.float32)
-
-    mine = (lax.broadcasted_iota(jnp.int32, (members, members * n_ens), 1)
-            == lax.broadcasted_iota(jnp.int32, (members, members * n_ens), 0) + me_ens * members)
-    noise = lax.dot_general(mine.astype(jnp.float32), noise_ref[0], NT, precision=HIGH,
-                            preferred_element_type=jnp.float32)
-    target = data_ref[...] + noise
-    inv_spread = lax.rsqrt(var_ref[...])
-
-    @pl.when(jnp.logical_not(last))
-    def _():
-        coef_up.wait_recv()
-        state_up.wait_recv()
-
-    @pl.when(jnp.logical_not(first))
-    def _():
-        coef_down.wait_recv()
-        state_down.wait_recv()
-
     lane = lax.broadcasted_iota(jnp.int32, (8, cols), 1)
 
-    @pl.loop(0, (rows + 2 * PAD) // 8)
-    def _(k):
-        at = pl.ds(pl.multiple_of(k * 8, 8), 8)
+    def build(at):
+        at = pl.ds(at, 8)
         d = craw[0, at, :] * FINE_DT
         hx = craw[1, at, :] * (0.5 * FINE_DT)
         hy = craw[2, at, :] * (0.5 * FINE_DT)
@@ -139,6 +118,46 @@
         ]
         cf[at] = jnp.swapaxes(jnp.stack(parts, axis=0), 0, 1)
 
+    def prepare(pair):
+        for side in (0, 1):
+            start_in(pair, side).wait()
+            at = block_of(pair, side)
+            st[pl.ds(PAD + at, 8)] = jnp.swapaxes(start_ref[:, pl.ds(at, 8), :], 0, 1)
+            build(PAD + at if isinstance(pair, int) else pl.multiple_of(PAD + at, 8))
+
+    small[0].wait()
+    pick = (lax.broadcasted_iota(jnp.int32, (bands, cols), 1) // (cols // bands)
+            == lax.broadcasted_iota(jnp.int32, (bands, cols), 0)).astype(jnp.float32)
+    par[...] = jnp.dot(params_ref[...], pick, precision=HIGH, preferred_element_type=jnp.float32)
+    pall[me_ens] = params_ref[...]
+    for k in range(4):
+        coef_in(k).wait()
+    prepare(0)
+
+    @pl.when(first)
+    def _():
+        craw[:, 0:PAD, :] = jnp.zeros((4, PAD, cols), jnp.float32)
+        st[0:PAD] = jnp.zeros((PAD, members, cols), jnp.float32)
+        rv[0] = jnp.zeros((members, cols), jnp.float32)
+
+    @pl.when(last)
+    def _():
+        craw[:, PAD + rows:, :] = jnp.zeros((4, PAD, cols), jnp.float32)
+        st[PAD + rows:] = jnp.zeros((PAD, members, cols), jnp.float32)
+        rv[rows + 1] = jnp.zeros((members, cols), jnp.float32)
+
+    pl.semaphore_wait(barrier, len(greeted))
+    share_params = remote(params_ref, pall.at[me_ens], ens_send.at[0], ens_recv.at[0], {"ens": other})
+    share_params.start()
+
+    @pl.when(jnp.logical_not(first))
+    def _():
+        coef_up.start()
+
+    @pl.when(jnp.logical_not(last))
+    def _():
+        coef_down.start()
+
     def spread(row, above, middle, below):
         c = [cf[row + PAD, k:k + 1, :] for k in range(5)]
         return (c[0] * middle + c[1] * above + c[2] * below
@@ -150,6 +169,10 @@
         force = cf[at, 5:6, :] * par[...]
         return middle + (spread(row, field[at - 1], middle, field[at + 1]) + force)
 
+    def coarse(row):
+        above, middle, below = (rv[row + k] - st[row + PAD - 1 + k] for k in range(3))
+        return middle + spread(row, above, middle, below) * float(FINE)
+
     def row_copy(row):
         return remote(nw.at[row], rv.at[row + 1], row_send.at[row], row_recv.at[row], {"tm": next_tm})
 
@@ -157,36 +180,51 @@
                      {"tm": next_tm, "space": up_sp})
     edge_down = remote(nw.at[rows - 1], rv.at[0], edge_send.at[1], edge_recv.at[1],
                        {"tm": next_tm, "space": dn_sp})
-    sends = me_tm < n_tm - 1
-    receives = me_tm > 0
-
-    def coarse(row):
-        above, middle, below = (rv[row + k] - st[row + PAD - 1 + k] for k in range(3))
-        return middle + spread(row, above, middle, below) * float(FINE)
-
-    @pl.loop(0, half + 6)
-    def _(step):
-        t = step - 3
-        for top in (True, False):
-            def place(r):
-                return r if top else rows - 1 - r
-            a1[place(t) + PAD] = fine(st, place(t))
-            a2[place(t - 1) + PAD] = fine(a1, place(t - 1))
-            a3[place(t - 2) + PAD] = fine(a2, place(t - 2))
+
+    def both(away):
+        return half - 1 - away, half + away
+
+    def finish(pair):
+        for side in (0, 1):
+            at = block_of(pair, side)
+            out_ref[:, pl.ds(at, 8), :] = jnp.swapaxes(nw[pl.ds(at, 8)], 0, 1)
+            result_out(pair, side).start()
+
+    def fine_both(field, away):
+        return [fine(field, row) for row in both(away)]
+
+    def keep(field, away, values):
+        for row, value in zip(both(away), values):
+            field[row + PAD] = value
+
+    @pl.loop(0, half + 3)
+    def _(t):
+        keep(a1, t, fine_both(st, t))
+        keep(a2, t - 1, fine_both(a1, t - 1))
+        keep(a3, t - 2, fine_both(a2, t - 2))
         q = t - 3
 
         @pl.when(q >= 0)
         def _():
-            nw[q] = fine(a3, q)
-            nw[rows - 1 - q] = fine(a3, rows - 1 - q)
+            upper, lower = both(q)
+            values = fine_both(a3, q)
+            nw[upper] = values[0]
+            nw[lower] = values[1]
 
             @pl.when(receives)
             def _():
                 @pl.when(q == 0)
                 def _():
-                    row_copy(0).wait_recv()
-                    row_copy(rows - 1).wait_recv()
-
+                    row_copy(half - 1).wait_recv()
+                    row_copy(half).wait_recv()
+
+                @pl.when(q < half - 1)
+                def _():
+                    row_copy(upper - 1).wait_recv()
+                    row_copy(lower + 1).wait_recv()
+
+                @pl.when(q == half - 1)
+                def _():
                     @pl.when(jnp.logical_not(last))
                     def _():
                         edge_up.wait_recv()
@@ -195,17 +233,13 @@
                     def _():
                         edge_down.wait_recv()
 
-                @pl.when(q < half - 1)
-                def _():
-                    row_copy(q + 1).wait_recv()
-                    row_copy(rows - 2 - q).wait_recv()
-
-                nw[q] = nw[q] + coarse(q)
-                nw[rows - 1 - q] = nw[rows - 1 - q] + coarse(rows - 1 - q)
+                more = [coarse(upper), coarse(lower)]
+                nw[upper] = nw[upper] + more[0]
+                nw[lower] = nw[lower] + more[1]
 
             @pl.when(sends)
             def _():
-                @pl.when(q == 0)
+                @pl.when(q == half - 1)
                 def _():
                     @pl.when(jnp.logical_not(first))
                     def _():
@@ -215,8 +249,50 @@
                     def _():
                         edge_down.start()
 
-                row_copy(q).start()
-                row_copy(rows - 1 - q).start()
+                row_copy(upper).start()
+                row_copy(lower).start()
+
+            @pl.when(jnp.logical_and(lax.rem(q, 8) == 7, q < half - 1))
+            def _():
+                finish(q // 8)
+
+        @pl.when(jnp.logical_and(lax.rem(t, 8) == 6, t < half - 2))
+        def _():
+            prepare((t + 2) // 8)
+
+        @pl.when(t == half - 9)
+        def _():
+            @pl.when(jnp.logical_not(first))
+            def _():
+                state_up.start()
+
+            @pl.when(jnp.logical_not(last))
+            def _():
+                state_down.start()
+
+        @pl.when(t == half - 2)
+        def _():
+            @pl.when(jnp.logical_not(last))
+            def _():
+                coef_up.wait_recv()
+                state_up.wait_recv()
+
+            @pl.when(jnp.logical_not(first))
+            def _():
+                coef_down.wait_recv()
+                state_down.wait_recv()
+
+            build(0)
+            build(PAD + rows)
+
+    for copy in small[1:]:
+        copy.wait()
+    mine = (lax.broadcasted_iota(jnp.int32, (members, members * n_ens), 1)
+            == lax.broadcasted_iota(jnp.int32, (members, members * n_ens), 0) + me_ens * members)
+    noise = lax.dot_general(mine.astype(jnp.float32), noise_ref[...], (((1,), (0,)), ((), ())),
+                            precision=HIGH, preferred_element_type=jnp.float32)
+    target = data_ref[...] + noise
+    inv_spread = lax.rsqrt(var_ref[...])
 
     lanes = lax.broadcasted_iota(jnp.int32, (members, 128), 1)
     wide = lax.broadcasted_iota(jnp.int32, (members, cols), 1)
@@ -235,11 +311,7 @@
     share_pred = remote(xall.at[me_ens], xall.at[me_ens], ens_send.at[1], ens_recv.at[1], {"ens": other})
     share_pred.start()
 
-    @pl.loop(0, rows // 8)
-    def _(k):
-        at = pl.multiple_of(k * 8, 8)
-        out_ref[:, pl.ds(at, 8), :] = jnp.swapaxes(nw[pl.ds(at, 8)], 0, 1)
-
+    finish(pairs - 1)
     share_pred.wait()
     total = members * n_ens
     norm_factor = 1.0 / math.sqrt(total - 1)
@@ -281,6 +353,10 @@
     own = jnp.where(me_ens == 0, update[:members], update[members:])
     new_params_ref[...] = params_ref[...] + own
 
+    for pair in range(pairs):
+        for side in (0, 1):
+            result_out(pair, side).wait()
+
     @pl.when(jnp.logical_not(first))
     def _():
         coef_up.wait_send()
@@ -320,13 +396,22 @@
     padded = (rows + 2 * PAD, members, cols)
     f32 = jnp.float32
     vmem = pl.BlockSpec(memory_space=pltpu.VMEM)
+    hbm = pl.BlockSpec(memory_space=pl.ANY)
     dma = pltpu.SemaphoreType.DMA
+    pairs = rows // 16
     new_states, new_params = pl.pallas_call(
         functools.partial(kernel, sizes),
         out_shape=(jax.ShapeDtypeStruct(state.shape, f32), jax.ShapeDtypeStruct(params.shape, f32)),
-        in_specs=[vmem] * 6 + [pl.BlockSpec(memory_space=pltpu.SMEM)] + [vmem] * 3,
-        out_specs=(vmem, vmem),
+        in_specs=[hbm] * 10,
+        out_specs=(hbm, vmem),
         scratch_shapes=[
+            pltpu.VMEM(state.shape, f32),
+            pltpu.VMEM(state.shape, f32),
+            pltpu.VMEM(params.shape, f32),
+            pltpu.SMEM(obs_cell.shape, jnp.int32),
+            pltpu.VMEM(obs_data.shape, f32),
+            pltpu.VMEM((total, obs_data.shape[1]), f32),
+            pltpu.VMEM(obs_var.shape, f32),
             pltpu.VMEM(padded, f32),
             pltpu.VMEM(padded, f32),
             pltpu.VMEM(padded, f32),
@@ -340,6 +425,7 @@
             pltpu.VMEM((n_ens, members, 128), f32),
             pltpu.VMEM((n_tm, total, 128), f32),
             pltpu.VMEM((n_sp, total, 128), f32),
+            dma((4,)), dma((5,)), dma((2, pairs)), dma((2, pairs)),
             dma((4,)), dma((4,)),
             dma((rows,)), dma((rows,)),
             dma((2,)), dma((2,)),
@@ -348,10 +434,10 @@
             dma((n_sp,)), dma((n_sp,)),
         ],
         compiler_params=pltpu.CompilerParams(
-            collective_id=0, has_side_effects=True, vmem_limit_bytes=48 * 2**20
+            collective_id=0, has_side_effects=True, vmem_limit_bytes=60 * 2**20
         ),
     )(state, velocity_x, velocity_y, diffusivity, source_shape, params,
-      obs_cell, obs_data, obs_noise, obs_var)
+      obs_cell, obs_data, jnp.swapaxes(obs_noise[0], 0, 1), obs_var)
     return (new_states[None], new_params)
 
 

time: 99.3 us -> 86.9 us (0.88)
  local copies, waits for them, and re-layouts: 10.7 us -> 3.76 us
  Pallas kernels: 87.6 us -> 82.4 us
    unnamed x21 -> x4, local copies, waits for them, and re-layouts: 10.7 us -> 3.76 us
    pallas_call x1, Pallas kernels: 87.6 us -> 82.4 us  [per_device(): pl.pallas_call(functools.partial(kernel, sizes), out_shape=(jax.ShapeDtyp...]
where the time goes in v2:
time: 86.9 us; the launch traced here: 86.8 us
  Pallas kernels  82.4 us (95%)
  local copies, waits for them, and re-layouts  3.76 us (4%)
    pallas_call x1, Pallas kernels, per_device(): pl.pallas_call(functools.partial(kernel, sizes), out_shape=(jax.ShapeDtyp...  82.4 us
    unnamed x4, local copies, waits for them, and re-layouts  3.76 us

profile of v2, /device:TPU:0, one launch (start us, length us, event | category | flops | bytes accessed | tf_op | source)
XLA Modules:
  0.0 86.8 jit_solution(17709588134955595611)
XLA Ops:
  0.6 82.4 %shard_map.113 = (f32[8,64,1024]{2,1,0:T(8,128)}, f32[8,128]{1,0:T(8,128)}) custom-call(f32[8,64,1024]{2,1,0:T(8,128)} %bitcast.5, f32[64,1024]{1,0:T(8,128)} %vx_hbm.1, f32[64,1024]{1,0:T(8,128)} %vy_hbm.1, f32[64,1024]{1,0:T(8,128)} %diff_hbm.1, f32[64,1024]{1,0:T(8,128)} %src_hbm.1, f32[8,128]{1,0:T(8,128)} %params_hbm.1, s32[1,64]{1,0:T(1,128)} %cell_hbm.1, ...), custom_call_target="tpu_custom_call" | custom-call | tf_op jit(solution)/shard_map/pallas_call | solution.py:402
  83.0 0.0 copy-start
  83.0 3.2 %copy.14 = f32[1,8,64,1024]{3,2,1,0:T(8,128)} copy(f32[1,8,64,1024]{3,2,1,0:T(8,128)} %bitcast.6) | data formatting | bytes 4194304
  86.2 0.0 copy-done
  86.2 0.6 copy.15
Async XLA Ops:
  83.0 3.2 %copy-start = (f32[8,128]{1,0:T(8,128)S(1)}, f32[8,128]{1,0:T(8,128)}, u32[]{:S(2)}) copy-start(f32[8,128]{1,0:T(8,128)} %get-tuple-element.9) | copy-start | bytes 12292

commit v3 on v2

--- a/solution.py
+++ b/solution.py
@@ -11,6 +11,7 @@
 FINE = 4
 FINE_DT = 0.25
 PAD = 8
+AHEAD = 3
 MESH = pl.DeviceIdType.MESH
 HIGH = lax.Precision.HIGHEST
 NT = (((1,), (1,)), ((), ()))
@@ -21,12 +22,12 @@
     sizes,
     start_hbm, vx_hbm, vy_hbm, diff_hbm, src_hbm, params_hbm,
     cell_hbm, data_hbm, noise_hbm, var_hbm,
-    out_hbm, new_params_ref,
-    start_ref, out_ref, params_ref, cell_ref, data_ref, noise_ref, var_ref,
-    st, a1, a2, a3, nw, rv, craw, cf, par, pall, xall, gtm, gsp,
-    in_sem, small_sem, block_sem, out_sem,
+    out_ref, new_params_ref,
+    start_ref, params_ref, cell_ref, data_ref, noise_ref, var_ref,
+    st, a1, a2, a3, nw, rv, craw, cf, par, pall, xall, sums,
+    in_sem, small_sem, block_sem,
     halo_send, halo_recv, row_send, row_recv, edge_send, edge_recv,
-    ens_send, ens_recv, tm_send, tm_recv, sp_send, sp_recv,
+    ens_send, ens_recv, sum_send, sum_recv,
 ):
     n_tm, n_sp, n_ens = sizes
     me_tm = lax.axis_index("tm")
@@ -42,7 +43,6 @@
     up_sp = lax.rem(me_sp + n_sp - 1, n_sp)
     dn_sp = lax.rem(me_sp + 1, n_sp)
     next_tm = lax.rem(me_tm + 1, n_tm)
-    prev_tm = lax.rem(me_tm + n_tm - 1, n_tm)
     sends = me_tm < n_tm - 1
     receives = me_tm > 0
 
@@ -57,10 +57,6 @@
     def coef_in(k):
         ref = (diff_hbm, vx_hbm, vy_hbm, src_hbm)[k]
         return pltpu.make_async_copy(ref, craw.at[k, pl.ds(PAD, rows)], in_sem.at[k])
-
-    def result_out(pair, side):
-        at = pl.ds(block_of(pair, side), 8)
-        return pltpu.make_async_copy(out_ref.at[:, at], out_hbm.at[:, at], out_sem.at[side, pair])
 
     small = [
         pltpu.make_async_copy(src, dst, small_sem.at[k])
@@ -79,10 +75,9 @@
         start_in(pair, 1).start()
 
     barrier = pltpu.get_barrier_semaphore()
-    greeted = [{"ens": other}]
-    greeted += [{"tm": lax.rem(me_tm + k, n_tm)} for k in range(1, n_tm)]
-    greeted += [{"space": lax.rem(me_sp + k, n_sp)} for k in range(1, n_sp)]
-    greeted += [{"tm": t, "space": s} for t in (next_tm, prev_tm) for s in (up_sp, dn_sp)]
+    chips = [(lax.rem(me_tm + t, n_tm), lax.rem(me_sp + z, n_sp))
+             for t in range(n_tm) for z in range(n_sp) if t or z]
+    greeted = [{"ens": other}] + [{"tm": t, "space": z} for t, z in chips]
     for device in greeted:
         pl.semaphore_signal(barrier, inc=1, device_id=device, device_id_type=MESH)
 
@@ -146,18 +141,6 @@
         st[PAD + rows:] = jnp.zeros((PAD, members, cols), jnp.float32)
         rv[rows + 1] = jnp.zeros((members, cols), jnp.float32)
 
-    pl.semaphore_wait(barrier, len(greeted))
-    share_params = remote(params_ref, pall.at[me_ens], ens_send.at[0], ens_recv.at[0], {"ens": other})
-    share_params.start()
-
-    @pl.when(jnp.logical_not(first))
-    def _():
-        coef_up.start()
-
-    @pl.when(jnp.logical_not(last))
-    def _():
-        coef_down.start()
-
     def spread(row, above, middle, below):
         c = [cf[row + PAD, k:k + 1, :] for k in range(5)]
         return (c[0] * middle + c[1] * above + c[2] * below
@@ -188,7 +171,6 @@
         for side in (0, 1):
             at = block_of(pair, side)
             out_ref[:, pl.ds(at, 8), :] = jnp.swapaxes(nw[pl.ds(at, 8)], 0, 1)
-            result_out(pair, side).start()
 
     def fine_both(field, away):
         return [fine(field, row) for row in both(away)]
@@ -197,7 +179,25 @@
         for row, value in zip(both(away), values):
             field[row + PAD] = value
 
-    @pl.loop(0, half + 3)
+    @pl.loop(0, FINE - 1)
+    def _(t):
+        keep(a1, t, fine_both(st, t))
+        keep(a2, t - 1, fine_both(a1, t - 1))
+        keep(a3, t - 2, fine_both(a2, t - 2))
+
+    pl.semaphore_wait(barrier, len(greeted))
+    share_params = remote(params_ref, pall.at[me_ens], ens_send.at[0], ens_recv.at[0], {"ens": other})
+    share_params.start()
+
+    @pl.when(jnp.logical_not(first))
+    def _():
+        coef_up.start()
+
+    @pl.when(jnp.logical_not(last))
+    def _():
+        coef_down.start()
+
+    @pl.loop(FINE - 1, half + 3)
     def _(t):
         keep(a1, t, fine_both(st, t))
         keep(a2, t - 1, fine_both(a1, t - 1))
@@ -248,6 +248,11 @@
                     @pl.when(jnp.logical_not(last))
                     def _():
                         edge_down.start()
+
+                @pl.when(q >= AHEAD)
+                def _():
+                    row_copy(upper + AHEAD).wait_send()
+                    row_copy(lower - AHEAD).wait_send()
 
                 row_copy(upper).start()
                 row_copy(lower).start()
@@ -318,25 +323,21 @@
     everyone = jnp.concatenate([xall[e] for e in range(n_ens)], axis=0)
     scaled, misfit = everyone[:, :n_obs], everyone[:, n_obs:]
     anomaly = (scaled - jnp.mean(scaled, axis=0, keepdims=True)) * norm_factor
+    here = me_tm * n_sp + me_sp
     right = jnp.concatenate(
         [anomaly, misfit, jnp.zeros((128 - 2 * total, n_obs), jnp.float32)], axis=0)
-    gtm[me_tm] = lax.dot_general(anomaly, right, NT, precision=HIGH,
+    sums[here] = lax.dot_general(anomaly, right, NT, precision=HIGH,
                                  preferred_element_type=jnp.float32)
 
-    def add_up(buffer, axis, me, count, send, recv):
-        peers = [lax.rem(me + k, count) for k in range(1, count)]
-        for peer in peers:
-            remote(buffer.at[me], buffer.at[me], send.at[peer], recv.at[me], {axis: peer}).start()
-        for peer in peers:
-            remote(buffer.at[peer], buffer.at[peer], send.at[peer], recv.at[peer], {axis: peer}).wait_recv()
-        summed = buffer[0]
-        for k in range(1, count):
-            summed = summed + buffer[k]
-        return summed, peers
-
-    summed, tm_peers = add_up(gtm, "tm", me_tm, n_tm, tm_send, tm_recv)
-    gsp[me_sp] = summed
-    system, sp_peers = add_up(gsp, "space", me_sp, n_sp, sp_send, sp_recv)
+    def sum_copy(slot, t, z):
+        return remote(sums.at[slot], sums.at[slot], sum_send.at[t * n_sp + z], sum_recv.at[slot],
+                      {"tm": t, "space": z})
+
+    for t, z in chips:
+        sum_copy(here, t, z).start()
+    for t, z in chips:
+        sum_copy(t * n_sp + z, t, z).wait_recv()
+    system = jnp.sum(sums[...], axis=0)
 
     row_no = lax.broadcasted_iota(jnp.int32, (total, 128), 0)
     system = system + (row_no == lax.broadcasted_iota(jnp.int32, (total, 128), 1)).astype(jnp.float32)
@@ -353,10 +354,6 @@
     own = jnp.where(me_ens == 0, update[:members], update[members:])
     new_params_ref[...] = params_ref[...] + own
 
-    for pair in range(pairs):
-        for side in (0, 1):
-            result_out(pair, side).wait()
-
     @pl.when(jnp.logical_not(first))
     def _():
         coef_up.wait_send()
@@ -377,14 +374,11 @@
         def _():
             edge_down.wait_send()
 
-        @pl.loop(0, rows)
-        def _(row):
+        for row in (*range(AHEAD), *range(rows - AHEAD, rows)):
             row_copy(row).wait_send()
 
-    for peer in tm_peers:
-        remote(gtm.at[me_tm], gtm.at[me_tm], tm_send.at[peer], tm_recv.at[me_tm], {"tm": peer}).wait_send()
-    for peer in sp_peers:
-        remote(gsp.at[me_sp], gsp.at[me_sp], sp_send.at[peer], sp_recv.at[me_sp], {"space": peer}).wait_send()
+    for t, z in chips:
+        sum_copy(here, t, z).wait_send()
 
 
 def per_device(sizes, start_states, velocity_x, velocity_y, diffusivity, source_shape, params,
@@ -403,9 +397,8 @@
         functools.partial(kernel, sizes),
         out_shape=(jax.ShapeDtypeStruct(state.shape, f32), jax.ShapeDtypeStruct(params.shape, f32)),
         in_specs=[hbm] * 10,
-        out_specs=(hbm, vmem),
+        out_specs=(vmem, vmem),
         scratch_shapes=[
-            pltpu.VMEM(state.shape, f32),
             pltpu.VMEM(state.shape, f32),
             pltpu.VMEM(params.shape, f32),
             pltpu.SMEM(obs_cell.shape, jnp.int32),
@@ -423,15 +416,13 @@
             pltpu.VMEM((members, cols), f32),
             pltpu.VMEM((n_ens,) + params.shape, f32),
             pltpu.VMEM((n_ens, members, 128), f32),
-            pltpu.VMEM((n_tm, total, 128), f32),
-            pltpu.VMEM((n_sp, total, 128), f32),
-            dma((4,)), dma((5,)), dma((2, pairs)), dma((2, pairs)),
+            pltpu.VMEM((n_tm * n_sp, total, 128), f32),
+            dma((4,)), dma((5,)), dma((2, pairs)),
             dma((4,)), dma((4,)),
             dma((rows,)), dma((rows,)),
             dma((2,)), dma((2,)),
             dma((2,)), dma((2,)),
-            dma((n_tm,)), dma((n_tm,)),
-            dma((n_sp,)), dma((n_sp,)),
+            dma((n_tm * n_sp,)), dma((n_tm * n_sp,)),
         ],
         compiler_params=pltpu.CompilerParams(
             collective_id=0, has_side_effects=True, vmem_limit_bytes=60 * 2**20

time: 86.9 us -> 85.2 us (0.980)
  Pallas kernels: 82.4 us -> 80.7 us
    pallas_call x1, Pallas kernels: 82.4 us -> 80.7 us  [per_device(): pl.pallas_call(functools.partial(kernel, sizes), out_shape=(jax.ShapeDtyp...]
where the time goes in v3:
time: 85.2 us; the launch traced here: 85.1 us
  Pallas kernels  80.7 us (95%)
  local copies, waits for them, and re-layouts  3.76 us (4%)
    pallas_call x1, Pallas kernels, per_device(): pl.pallas_call(functools.partial(kernel, sizes), out_shape=(jax.ShapeDtyp...  80.7 us
    unnamed x4, local copies, waits for them, and re-layouts  3.76 us

profile of v3, /device:TPU:0, one launch (start us, length us, event | category | flops | bytes accessed | tf_op | source)
XLA Modules:
  0.0 85.1 jit_solution(12214991271474807528)
XLA Ops:
  0.6 80.7 %shard_map.113 = (f32[8,64,1024]{2,1,0:T(8,128)}, f32[8,128]{1,0:T(8,128)}) custom-call(f32[8,64,1024]{2,1,0:T(8,128)} %bitcast.5, f32[64,1024]{1,0:T(8,128)} %vx_hbm.1, f32[64,1024]{1,0:T(8,128)} %vy_hbm.1, f32[64,1024]{1,0:T(8,128)} %diff_hbm.1, f32[64,1024]{1,0:T(8,128)} %src_hbm.1, f32[8,128]{1,0:T(8,128)} %params_hbm.1, s32[1,64]{1,0:T(1,128)} %cell_hbm.1, ...), custom_call_target="tpu_custom_call" | custom-call | tf_op jit(solution)/shard_map/pallas_call | solution.py:396
  81.3 0.0 copy-start
  81.3 3.2 %copy.14 = f32[1,8,64,1024]{3,2,1,0:T(8,128)} copy(f32[1,8,64,1024]{3,2,1,0:T(8,128)} %bitcast.6) | data formatting | bytes 4194304
  84.5 0.0 copy-done
  84.5 0.6 copy.15
Async XLA Ops:
  81.3 3.2 %copy-start = (f32[8,128]{1,0:T(8,128)S(1)}, f32[8,128]{1,0:T(8,128)}, u32[]{:S(2)}) copy-start(f32[8,128]{1,0:T(8,128)} %get-tuple-element.9) | copy-start | bytes 12292

commit v4 on v3

--- a/solution.py
+++ b/solution.py
@@ -179,11 +179,16 @@
         for row, value in zip(both(away), values):
             field[row + PAD] = value
 
-    @pl.loop(0, FINE - 1)
-    def _(t):
-        keep(a1, t, fine_both(st, t))
-        keep(a2, t - 1, fine_both(a1, t - 1))
-        keep(a3, t - 2, fine_both(a2, t - 2))
+    fields = (st, a1, a2, a3)
+
+    def fine_steps(t, count):
+        for k in reversed(range(count)):
+            keep(fields[k + 1], t - 2 * k, fine_both(fields[k], t - 2 * k))
+
+    for count in range(1, FINE):
+        @pl.loop(2 * count - 2, 2 * count)
+        def _(t):
+            fine_steps(t, count)
 
     pl.semaphore_wait(barrier, len(greeted))
     share_params = remote(params_ref, pall.at[me_ens], ens_send.at[0], ens_recv.at[0], {"ens": other})
@@ -196,99 +201,6 @@
     @pl.when(jnp.logical_not(last))
     def _():
         coef_down.start()
-
-    @pl.loop(FINE - 1, half + 3)
-    def _(t):
-        keep(a1, t, fine_both(st, t))
-        keep(a2, t - 1, fine_both(a1, t - 1))
-        keep(a3, t - 2, fine_both(a2, t - 2))
-        q = t - 3
-
-        @pl.when(q >= 0)
-        def _():
-            upper, lower = both(q)
-            values = fine_both(a3, q)
-            nw[upper] = values[0]
-            nw[lower] = values[1]
-
-            @pl.when(receives)
-            def _():
-                @pl.when(q == 0)
-                def _():
-                    row_copy(half - 1).wait_recv()
-                    row_copy(half).wait_recv()
-
-                @pl.when(q < half - 1)
-                def _():
-                    row_copy(upper - 1).wait_recv()
-                    row_copy(lower + 1).wait_recv()
-
-                @pl.when(q == half - 1)
-                def _():
-                    @pl.when(jnp.logical_not(last))
-                    def _():
-                        edge_up.wait_recv()
-
-                    @pl.when(jnp.logical_not(first))
-                    def _():
-                        edge_down.wait_recv()
-
-                more = [coarse(upper), coarse(lower)]
-                nw[upper] = nw[upper] + more[0]
-                nw[lower] = nw[lower] + more[1]
-
-            @pl.when(sends)
-            def _():
-                @pl.when(q == half - 1)
-                def _():
-                    @pl.when(jnp.logical_not(first))
-                    def _():
-                        edge_up.start()
-
-                    @pl.when(jnp.logical_not(last))
-                    def _():
-                        edge_down.start()
-
-                @pl.when(q >= AHEAD)
-                def _():
-                    row_copy(upper + AHEAD).wait_send()
-                    row_copy(lower - AHEAD).wait_send()
-
-                row_copy(upper).start()
-                row_copy(lower).start()
-
-            @pl.when(jnp.logical_and(lax.rem(q, 8) == 7, q < half - 1))
-            def _():
-                finish(q // 8)
-
-        @pl.when(jnp.logical_and(lax.rem(t, 8) == 6, t < half - 2))
-        def _():
-            prepare((t + 2) // 8)
-
-        @pl.when(t == half - 9)
-        def _():
-            @pl.when(jnp.logical_not(first))
-            def _():
-                state_up.start()
-
-            @pl.when(jnp.logical_not(last))
-            def _():
-                state_down.start()
-
-        @pl.when(t == half - 2)
-        def _():
-            @pl.when(jnp.logical_not(last))
-            def _():
-                coef_up.wait_recv()
-                state_up.wait_recv()
-
-            @pl.when(jnp.logical_not(first))
-            def _():
-                coef_down.wait_recv()
-                state_down.wait_recv()
-
-            build(0)
-            build(PAD + rows)
 
     for copy in small[1:]:
         copy.wait()
@@ -298,6 +210,96 @@
                             precision=HIGH, preferred_element_type=jnp.float32)
     target = data_ref[...] + noise
     inv_spread = lax.rsqrt(var_ref[...])
+
+    delay = 2 * (FINE - 1)
+
+    @pl.loop(delay, half + delay)
+    def _(t):
+        q = t - delay
+        upper, lower = both(q)
+        values = fine_both(a3, q)
+        nw[upper] = values[0]
+        nw[lower] = values[1]
+        fine_steps(t, FINE - 1)
+
+        @pl.when(receives)
+        def _():
+            @pl.when(q == 0)
+            def _():
+                row_copy(half - 1).wait_recv()
+                row_copy(half).wait_recv()
+
+            @pl.when(q < half - 1)
+            def _():
+                row_copy(upper - 1).wait_recv()
+                row_copy(lower + 1).wait_recv()
+
+            @pl.when(q == half - 1)
+            def _():
+                @pl.when(jnp.logical_not(last))
+                def _():
+                    edge_up.wait_recv()
+
+                @pl.when(jnp.logical_not(first))
+                def _():
+                    edge_down.wait_recv()
+
+            more = [coarse(upper), coarse(lower)]
+            nw[upper] = nw[upper] + more[0]
+            nw[lower] = nw[lower] + more[1]
+
+        @pl.when(sends)
+        def _():
+            @pl.when(q == half - 1)
+            def _():
+                @pl.when(jnp.logical_not(first))
+                def _():
+                    edge_up.start()
+
+                @pl.when(jnp.logical_not(last))
+                def _():
+                    edge_down.start()
+
+            @pl.when(q >= AHEAD)
+            def _():
+                row_copy(upper + AHEAD).wait_send()
+                row_copy(lower - AHEAD).wait_send()
+
+            row_copy(upper).start()
+            row_copy(lower).start()
+
+        @pl.when(jnp.logical_and(lax.rem(q, 8) == 7, q < half - 1))
+        def _():
+            finish(q // 8)
+
+        @pl.when(jnp.logical_and(lax.rem(t, 8) == 6, t < half - 2))
+        def _():
+            prepare((t + 2) // 8)
+
+        @pl.when(t == half - 9)
+        def _():
+            @pl.when(jnp.logical_not(first))
+            def _():
+                state_up.start()
+
+            @pl.when(jnp.logical_not(last))
+            def _():
+                state_down.start()
+
+        @pl.when(t == half - 2)
+        def _():
+            @pl.when(jnp.logical_not(last))
+            def _():
+                coef_up.wait_recv()
+                state_up.wait_recv()
+
+            @pl.when(jnp.logical_not(first))
+            def _():
+                coef_down.wait_recv()
+                state_down.wait_recv()
+
+            build(0)
+            build(PAD + rows)
 
     lanes = lax.broadcasted_iota(jnp.int32, (members, 128), 1)
     wide = lax.broadcasted_iota(jnp.int32, (members, cols), 1)

time: 85.2 us -> 84.9 us (level)
  no operation moved by 1% of the time
where the time goes in v4:
time: 84.9 us; the launch traced here: 84.8 us
  Pallas kernels  80.4 us (95%)
  local copies, waits for them, and re-layouts  3.76 us (4%)
    pallas_call x1, Pallas kernels, per_device(): pl.pallas_call(functools.partial(kernel, sizes), out_shape=(jax.ShapeDtyp...  80.4 us
    unnamed x4, local copies, waits for them, and re-layouts  3.76 us

profile of v4, /device:TPU:0, one launch (start us, length us, event | category | flops | bytes accessed | tf_op | source)
XLA Modules:
  0.0 84.8 jit_solution(1335136878356538676)
XLA Ops:
  0.6 80.4 %shard_map.113 = (f32[8,64,1024]{2,1,0:T(8,128)}, f32[8,128]{1,0:T(8,128)}) custom-call(f32[8,64,1024]{2,1,0:T(8,128)} %bitcast.5, f32[64,1024]{1,0:T(8,128)} %vx_hbm.1, f32[64,1024]{1,0:T(8,128)} %vy_hbm.1, f32[64,1024]{1,0:T(8,128)} %diff_hbm.1, f32[64,1024]{1,0:T(8,128)} %src_hbm.1, f32[8,128]{1,0:T(8,128)} %params_hbm.1, s32[1,64]{1,0:T(1,128)} %cell_hbm.1, ...), custom_call_target="tpu_custom_call" | custom-call | tf_op jit(solution)/shard_map/pallas_call | solution.py:398
  81.0 0.0 copy-start
  81.0 3.2 %copy.14 = f32[1,8,64,1024]{3,2,1,0:T(8,128)} copy(f32[1,8,64,1024]{3,2,1,0:T(8,128)} %bitcast.6) | data formatting | bytes 4194304
  84.2 0.0 copy-done
  84.2 0.6 copy.15
Async XLA Ops:
  81.0 3.2 %copy-start = (f32[8,128]{1,0:T(8,128)S(1)}, f32[8,128]{1,0:T(8,128)}, u32[]{:S(2)}) copy-start(f32[8,128]{1,0:T(8,128)} %get-tuple-element.9) | copy-start | bytes 12292

commit v5 on v4

--- a/solution.py
+++ b/solution.py
@@ -11,7 +11,7 @@
 FINE = 4
 FINE_DT = 0.25
 PAD = 8
-AHEAD = 3
+AHEAD = 8
 MESH = pl.DeviceIdType.MESH
 HIGH = lax.Precision.HIGHEST
 NT = (((1,), (1,)), ((), ()))
@@ -101,17 +101,20 @@
     lane = lax.broadcasted_iota(jnp.int32, (8, cols), 1)
 
     def build(at):
-        at = pl.ds(at, 8)
-        d = craw[0, at, :] * FINE_DT
-        hx = craw[1, at, :] * (0.5 * FINE_DT)
-        hy = craw[2, at, :] * (0.5 * FINE_DT)
+        rows_at = pl.ds(at, 8)
+        d = craw[0, rows_at, :] * FINE_DT
+        hx = craw[1, rows_at, :] * (0.5 * FINE_DT)
+        hy = craw[2, rows_at, :] * (0.5 * FINE_DT)
         parts = [
             -4.0 * d, d + hy, d - hy,
             jnp.where(lane == 0, 0.0, d + hx),
             jnp.where(lane == cols - 1, 0.0, d - hx),
-            craw[3, at, :] * FINE_DT, d, d,
+            craw[3, rows_at, :] * FINE_DT,
         ]
-        cf[at] = jnp.swapaxes(jnp.stack(parts, axis=0), 0, 1)
+        for i in range(8):
+            for k, part in enumerate(parts):
+                spread_out = jnp.broadcast_to(part[i:i + 1, :], (members, cols))
+                cf[at + i, k] = spread_out * par[...] if k == 5 else spread_out
 
     def prepare(pair):
         for side in (0, 1):
@@ -142,15 +145,14 @@
         rv[rows + 1] = jnp.zeros((members, cols), jnp.float32)
 
     def spread(row, above, middle, below):
-        c = [cf[row + PAD, k:k + 1, :] for k in range(5)]
+        c = [cf[row + PAD, k] for k in range(5)]
         return (c[0] * middle + c[1] * above + c[2] * below
                 + c[3] * pltpu.roll(middle, 1, 1) + c[4] * pltpu.roll(middle, cols - 1, 1))
 
     def fine(field, row):
         at = row + PAD
         middle = field[at]
-        force = cf[at, 5:6, :] * par[...]
-        return middle + (spread(row, field[at - 1], middle, field[at + 1]) + force)
+        return middle + (spread(row, field[at - 1], middle, field[at + 1]) + cf[at, 5])
 
     def coarse(row):
         above, middle, below = (rv[row + k] - st[row + PAD - 1 + k] for k in range(3))
@@ -414,7 +416,7 @@
             pltpu.VMEM((rows, members, cols), f32),
             pltpu.VMEM((rows + 2, members, cols), f32),
             pltpu.VMEM((4, rows + 2 * PAD, cols), f32),
-            pltpu.VMEM((rows + 2 * PAD, 8, cols), f32),
+            pltpu.VMEM((rows + 2 * PAD, 6, members, cols), f32),
             pltpu.VMEM((members, cols), f32),
             pltpu.VMEM((n_ens,) + params.shape, f32),
             pltpu.VMEM((n_ens, members, 128), f32),

time: 84.9 us -> 85.8 us (1.011)
    pallas_call x1, Pallas kernels: 80.4 us -> 81.2 us  [per_device(): pl.pallas_call(functools.partial(kernel, sizes), out_shape=(jax.ShapeDtyp...]
where the time goes in v5:
time: 85.8 us; the launch traced here: 85.6 us
  Pallas kernels  81.2 us (95%)
  local copies, waits for them, and re-layouts  3.76 us (4%)
    pallas_call x1, Pallas kernels, per_device(): pl.pallas_call(functools.partial(kernel, sizes), out_shape=(jax.ShapeDtyp...  81.2 us
    unnamed x4, local copies, waits for them, and re-layouts  3.76 us

profile of v5, /device:TPU:0, one launch (start us, length us, event | category | flops | bytes accessed | tf_op | source)
XLA Modules:
  0.0 85.6 jit_solution(1818331449604011214)
XLA Ops:
  0.6 81.2 %shard_map.113 = (f32[8,64,1024]{2,1,0:T(8,128)}, f32[8,128]{1,0:T(8,128)}) custom-call(f32[8,64,1024]{2,1,0:T(8,128)} %bitcast.5, f32[64,1024]{1,0:T(8,128)} %vx_hbm.1, f32[64,1024]{1,0:T(8,128)} %vy_hbm.1, f32[64,1024]{1,0:T(8,128)} %diff_hbm.1, f32[64,1024]{1,0:T(8,128)} %src_hbm.1, f32[8,128]{1,0:T(8,128)} %params_hbm.1, s32[1,64]{1,0:T(1,128)} %cell_hbm.1, ...), custom_call_target="tpu_custom_call" | custom-call | tf_op jit(solution)/shard_map/pallas_call | solution.py:400
  81.9 0.0 copy-start
  81.9 3.2 %copy.14 = f32[1,8,64,1024]{3,2,1,0:T(8,128)} copy(f32[1,8,64,1024]{3,2,1,0:T(8,128)} %bitcast.6) | data formatting | bytes 4194304
  85.0 0.0 copy-done
  85.1 0.6 copy.15
Async XLA Ops:
  81.9 3.2 %copy-start = (f32[8,128]{1,0:T(8,128)S(1)}, f32[8,128]{1,0:T(8,128)}, u32[]{:S(2)}) copy-start(f32[8,128]{1,0:T(8,128)} %get-tuple-element.9) | copy-start | bytes 12292

commit v6 on v4

--- a/solution.py
+++ b/solution.py
@@ -381,6 +381,21 @@
 
     for t, z in chips:
         sum_copy(here, t, z).wait_send()
+
+
+def hand_over(states_hbm, params_hbm, out_hbm, new_params_hbm, held, held_params, in_sem, out_sem):
+    count = states_hbm.shape[0]
+    pieces = [(states_hbm.at[k], held.at[k], out_hbm.at[k]) for k in range(count)]
+    pieces.append((params_hbm, held_params, new_params_hbm))
+    arriving = [pltpu.make_async_copy(src, mid, in_sem.at[k]) for k, (src, mid, _) in enumerate(pieces)]
+    leaving = [pltpu.make_async_copy(mid, dst, out_sem.at[k]) for k, (_, mid, dst) in enumerate(pieces)]
+    for copy in arriving:
+        copy.start()
+    for before, after in zip(arriving, leaving):
+        before.wait()
+        after.start()
+    for copy in leaving:
+        copy.wait()
 
 
 def per_device(sizes, start_states, velocity_x, velocity_y, diffusivity, source_shape, params,
@@ -431,6 +446,17 @@
         ),
     )(state, velocity_x, velocity_y, diffusivity, source_shape, params,
       obs_cell, obs_data, jnp.swapaxes(obs_noise[0], 0, 1), obs_var)
+    new_states, new_params = pl.pallas_call(
+        hand_over,
+        out_shape=(jax.ShapeDtypeStruct(state.shape, f32), jax.ShapeDtypeStruct(params.shape, f32)),
+        in_specs=[hbm] * 2,
+        out_specs=(hbm, hbm),
+        scratch_shapes=[
+            pltpu.VMEM(state.shape, f32), pltpu.VMEM(params.shape, f32),
+            dma((members + 1,)), dma((members + 1,)),
+        ],
+        compiler_params=pltpu.CompilerParams(vmem_limit_bytes=60 * 2**20),
+    )(new_states, new_params)
     return (new_states[None], new_params)
 
 

time: 84.9 us -> 83.6 us (0.985)
  local copies, waits for them, and re-layouts: 3.76 us -> 0 us
  Pallas kernels: 80.4 us -> 82.8 us
    unnamed x4 -> x0, local copies, waits for them, and re-layouts: 3.76 us -> none
    pallas_call x0 -> x1, Pallas kernels: none -> 2.41 us  [per_device(): pl.pallas_call(hand_over, out_shape=(jax.ShapeDtypeStruct(state.shape, f3...]
where the time goes in v6:
time: 83.6 us; the launch traced here: 83.4 us
  Pallas kernels  82.8 us (99%)
    pallas_call x1, Pallas kernels, per_device(): pl.pallas_call(functools.partial(kernel, sizes), out_shape=(jax.ShapeDtyp...  80.4 us
    pallas_call x1, Pallas kernels, per_device(): pl.pallas_call(hand_over, out_shape=(jax.ShapeDtypeStruct(state.shape, f3...  2.41 us

profile of v6, /device:TPU:0, one launch (start us, length us, event | category | flops | bytes accessed | tf_op | source)
XLA Modules:
  0.0 83.4 jit_solution(14166417653899592125)
XLA Ops:
  0.6 80.4 %shard_map.113 = (f32[8,64,1024]{2,1,0:T(8,128)}, f32[8,128]{1,0:T(8,128)}) custom-call(f32[8,64,1024]{2,1,0:T(8,128)} %bitcast.5, f32[64,1024]{1,0:T(8,128)} %vx_hbm.1, f32[64,1024]{1,0:T(8,128)} %vy_hbm.1, f32[64,1024]{1,0:T(8,128)} %diff_hbm.1, f32[64,1024]{1,0:T(8,128)} %src_hbm.1, f32[8,128]{1,0:T(8,128)} %params_hbm.1, s32[1,64]{1,0:T(1,128)} %cell_hbm.1, ...), custom_call_target="tpu_custom_call" | custom-call | tf_op jit(solution)/shard_map/pallas_call | solution.py:413
  81.0 2.4 %shard_map.114 = (f32[8,64,1024]{2,1,0:T(8,128)}, f32[8,128]{1,0:T(8,128)}) custom-call(f32[8,64,1024]{2,1,0:T(8,128)} %get-tuple-element.6.states_hbm, f32[8,128]{1,0:T(8,128)} %get-tuple-element.7.params_hbm), custom_call_target="tpu_custom_call" | custom-call | tf_op jit(solution)/shard_map/pallas_call | solution.py:449
